TPU v7x, 32 devices: a whole 2x2x4 slice. The times are simulated.
32 devices in a mesh: seq: 4 (over y, x), fsdp: 8 (over z, core).
Axes of the slice: x: 2, y: 2, z: 4, core: 2. Of those that a mesh axis runs over, the one named last changes fastest.
Arguments:
- block_input: bfloat16 [8, 1024, 1536], P('fsdp', 'seq'), may hold values from -6 to 6
- cotangent: bfloat16 [8, 1024, 1536], P('fsdp', 'seq'), may hold values from -6 to 6
- routes: int32 [8, 1024, 2], P('fsdp', 'seq'), may hold values from 0 to 3, all different within a row; in each aligned block of 256 rows (0 to 255, 256 to 511, ..., all dimensions but the last counted through in order) at most 192 rows name the same one
- gain_attn: bfloat16 [1536], P(('seq', 'fsdp')), may hold values from 0.099609375 to 1.8984375
- w_query: bfloat16 [1536, 1536], P(('seq', 'fsdp')), may hold values from -0.15625 to 0.15625
- w_key: bfloat16 [1536, 512], P(('seq', 'fsdp')), may hold values from -0.15625 to 0.15625
- w_value: bfloat16 [1536, 512], P(('seq', 'fsdp')), may hold values from -0.15625 to 0.15625
- w_out: bfloat16 [1536, 1536], P(('seq', 'fsdp')), may hold values from -1.75 to 1.75
- gain_ffn: bfloat16 [1536], P(('seq', 'fsdp')), may hold values from 0.099609375 to 1.8984375
- router: bfloat16 [1536, 4], P(('seq', 'fsdp')), may hold values from -0.119628906 to 0.119628906
- w_gate: bfloat16 [4, 1536, 1024], P(None, ('seq', 'fsdp')), may hold values from -0.15625 to 0.15625
- w_up: bfloat16 [4, 1536, 1024], P(None, ('seq', 'fsdp')), may hold values from -0.15625 to 0.15625
- w_down: bfloat16 [4, 1024, 1536], P(None, ('seq', 'fsdp')), may hold values from -0.1875 to 0.1875
Outputs:
- output: bfloat16 [8, 1024, 1536], P('fsdp', 'seq')
- grad_input: bfloat16 [8, 1024, 1536], P('fsdp', 'seq')
- grad_gain_attn: float32 [1536], P(('seq', 'fsdp'))
- grad_w_query: float32 [1536, 1536], P(('seq', 'fsdp'))
- grad_w_key: float32 [1536, 512], P(('seq', 'fsdp'))
- grad_w_value: float32 [1536, 512], P(('seq', 'fsdp'))
- grad_w_out: float32 [1536, 1536], P(('seq', 'fsdp'))
- grad_gain_ffn: float32 [1536], P(('seq', 'fsdp'))
- grad_router: float32 [1536, 4], P(('seq', 'fsdp'))
- grad_w_gate: float32 [4, 1536, 1024], P(None, ('seq', 'fsdp'))
- grad_w_up: float32 [4, 1536, 1024], P(None, ('seq', 'fsdp'))
- grad_w_down: float32 [4, 1024, 1536], P(None, ('seq', 'fsdp'))
Inputs may be any that keep to these rules, and one draw needn't show every extreme that they name: `routes`: each row names two different experts. Among the 256 rows of one device (aligned blocks of the sequence and position dimensions taken in order), no expert is named more than 192 times, and in some block one expert is named exactly 192 times.
All inputs are finite; a program needn't handle non-finite values.
Results may differ from a plain program's by a relative error of at most 0.014.
The roundings to bfloat16 on the way count: a program that leaves them out, or rounds other values in their place, can miss the bound.
Values may be sent and summed in bfloat16 or wider, within the bound.
A program may use at most 256 MiB of HBM per device.

v0:
```python
import jax
import jax.numpy as jnp
from jax import lax
from jax.sharding import PartitionSpec as P

HEADS = 24
KV_HEADS = 8
HEAD_DIM = 64


eps = 1e-06


def rms_factor(rows):
    return lax.rsqrt(jnp.mean(rows * rows, axis=-1, keepdims=True) + eps)


def score_block(query_block, keys, first_row, score_scale):
    block_rows = query_block.shape[0]
    length = keys.shape[0]
    scores = score_scale * jnp.einsum(
        "qgrd,kgd->grqk", query_block, keys, preferred_element_type=jnp.float32
    )
    row_index = first_row + jnp.arange(block_rows)
    allowed = jnp.arange(length)[None, :] <= row_index[:, None]
    return jnp.where(allowed, scores, -1e30)


def attention_forward(queries, keys, values, block_rows, score_scale):
    length = keys.shape[0]
    block_count = length // block_rows
    grouped = queries.reshape(
        block_count, block_rows, queries.shape[1], queries.shape[2], queries.shape[3]
    )

    def one_block(block_args):
        query_block, first_row = block_args
        scores = score_block(query_block, keys, first_row, score_scale)
        row_max = jnp.max(scores, axis=-1, keepdims=True)
        exponent = jnp.exp(scores - row_max)
        row_total = jnp.sum(exponent, axis=-1, keepdims=True)
        probability = (exponent / row_total).astype(jnp.bfloat16)
        result = jnp.einsum(
            "grqk,kgd->qgrd", probability, values, preferred_element_type=jnp.float32
        )
        return (result.astype(jnp.bfloat16), (row_max + jnp.log(row_total))[..., 0])

    starts = jnp.arange(block_count) * block_rows
    results, log_totals = lax.map(one_block, (grouped, starts))
    return (results.reshape(length, -1), log_totals)


def attention_backward(queries, keys, values, grad_heads, log_totals, block_rows, score_scale):
    length = keys.shape[0]
    block_count = length // block_rows
    grouped = queries.reshape(
        block_count, block_rows, queries.shape[1], queries.shape[2], queries.shape[3]
    )
    grad_grouped = grad_heads.reshape(grouped.shape)

    def one_block(running, block_args):
        grad_keys, grad_values = running
        query_block, grad_block, log_total, first_row = block_args
        scores = score_block(query_block, keys, first_row, score_scale)
        probability = jnp.exp(scores - log_total[..., None])
        grad_prob = jnp.einsum(
            "qgrd,kgd->grqk", grad_block, values, preferred_element_type=jnp.float32
        )
        row_delta = jnp.sum(probability * grad_prob, axis=-1, keepdims=True)
        grad_scores = (probability * (grad_prob - row_delta)).astype(jnp.bfloat16)
        grad_query = score_scale * jnp.einsum(
            "grqk,kgd->qgrd", grad_scores, keys, preferred_element_type=jnp.float32
        )
        grad_keys = grad_keys + score_scale * jnp.einsum(
            "grqk,qgrd->kgd", grad_scores, query_block, preferred_element_type=jnp.float32
        )
        grad_values = grad_values + jnp.einsum(
            "grqk,qgrd->kgd",
            probability.astype(jnp.bfloat16),
            grad_block,
            preferred_element_type=jnp.float32,
        )
        return ((grad_keys, grad_values), grad_query.astype(jnp.bfloat16))

    empty = jnp.zeros(keys.shape, jnp.float32)
    starts = jnp.arange(block_count) * block_rows
    (grad_keys, grad_values), grad_query = lax.scan(
        one_block, (empty, empty), (grouped, grad_grouped, log_totals, starts)
    )
    return (
        grad_query.reshape(length, -1),
        grad_keys.reshape(length, -1).astype(jnp.bfloat16),
        grad_values.reshape(length, -1).astype(jnp.bfloat16),
    )


def shards(
    block_input,
    cotangent,
    routes,
    gain_attn,
    w_query,
    w_key,
    w_value,
    w_out,
    gain_ffn,
    router,
    w_gate,
    w_up,
    w_down,
):
    gain_first, query_all, key_all, value_all, out_all, gain_second, router_all = (
        lax.all_gather(gain_attn, ("seq", "fsdp"), axis=0, tiled=True),
        lax.all_gather(w_query, ("seq", "fsdp"), axis=0, tiled=True),
        lax.all_gather(w_key, ("seq", "fsdp"), axis=0, tiled=True),
        lax.all_gather(w_value, ("seq", "fsdp"), axis=0, tiled=True),
        lax.all_gather(w_out, ("seq", "fsdp"), axis=0, tiled=True),
        lax.all_gather(gain_ffn, ("seq", "fsdp"), axis=0, tiled=True),
        lax.all_gather(router, ("seq", "fsdp"), axis=0, tiled=True),
    )
    gate_all, up_all, down_all = (
        lax.all_gather(w_gate, ("seq", "fsdp"), axis=1, tiled=True),
        lax.all_gather(w_up, ("seq", "fsdp"), axis=1, tiled=True),
        lax.all_gather(w_down, ("seq", "fsdp"), axis=1, tiled=True),
    )
    inputs = block_input[0].astype(jnp.float32)
    tokens = inputs.shape[0]
    factor_first = rms_factor(inputs)
    plain_first = inputs * factor_first
    gain_one = gain_first.astype(jnp.float32)
    normed1 = (plain_first * gain_one).astype(jnp.bfloat16)
    queries = jnp.dot(normed1, query_all, preferred_element_type=jnp.float32).astype(jnp.bfloat16)
    keys = jnp.dot(normed1, key_all, preferred_element_type=jnp.float32).astype(jnp.bfloat16)
    values = jnp.dot(normed1, value_all, preferred_element_type=jnp.float32).astype(jnp.bfloat16)
    query_cols, key_cols, value_cols = (
        lax.all_to_all(queries, "seq", split_axis=1, concat_axis=0, tiled=True),
        lax.all_to_all(keys, "seq", split_axis=1, concat_axis=0, tiled=True),
        lax.all_to_all(values, "seq", split_axis=1, concat_axis=0, tiled=True),
    )
    length = key_cols.shape[0]
    block_rows = min(512, length)
    heads_ratio = HEADS // KV_HEADS
    groups = key_cols.shape[1] // HEAD_DIM
    score_scale = HEAD_DIM ** (-0.5)
    query_heads = query_cols.reshape(length, groups, heads_ratio, HEAD_DIM)
    key_heads = key_cols.reshape(length, groups, HEAD_DIM)
    value_heads = value_cols.reshape(length, groups, HEAD_DIM)
    attn_heads, log_totals = attention_forward(
        query_heads, key_heads, value_heads, block_rows, score_scale
    )
    attn_tokens = lax.all_to_all(attn_heads, "seq", split_axis=0, concat_axis=1, tiled=True)
    mixed = inputs + jnp.dot(attn_tokens, out_all, preferred_element_type=jnp.float32)
    factor_second = rms_factor(mixed)
    plain_second = mixed * factor_second
    gain_two = gain_second.astype(jnp.float32)
    normed2 = (plain_second * gain_two).astype(jnp.bfloat16)
    logits = jnp.dot(normed2, router_all, preferred_element_type=jnp.float32)
    experts = router_all.shape[1]
    expert_ids = routes[0]
    choose = (expert_ids[:, :, None] == jnp.arange(experts)[None, None, :]).astype(jnp.float32)
    picked = jnp.sum(choose * logits[:, None, :], axis=-1)
    gate_values = jax.nn.softmax(picked, axis=-1)
    capacity = 3 * tokens // 4
    flat_ids = expert_ids.reshape(-1)
    onehot = (flat_ids[:, None] == jnp.arange(experts)[None, :]).astype(jnp.int32)
    earlier = jnp.cumsum(onehot, axis=0) - onehot
    slot_index = jnp.sum(earlier * onehot, axis=1)
    target = flat_ids * capacity + slot_index
    owner_token = jnp.arange(2 * tokens) // 2
    source = jnp.zeros((experts * capacity,), jnp.int32).at[target].set(owner_token)
    packed = normed2[source].reshape(experts, capacity, -1)
    gate_pre = jnp.einsum("ecd,edf->ecf", packed, gate_all, preferred_element_type=jnp.float32)
    up_pre = jnp.einsum("ecd,edf->ecf", packed, up_all, preferred_element_type=jnp.float32)
    sigmoid_gate = jax.nn.sigmoid(gate_pre)
    activated = gate_pre * sigmoid_gate
    hidden = (activated * up_pre).astype(jnp.bfloat16)
    expert_out = jnp.einsum(
        "ecf,efd->ecd", hidden, down_all, preferred_element_type=jnp.float32
    ).reshape(experts * capacity, -1)
    paired = expert_out[target].reshape(tokens, 2, -1)
    result = mixed + jnp.sum(gate_values[:, :, None] * paired, axis=1)
    output = result.astype(jnp.bfloat16)[None]
    upstream = cotangent[0].astype(jnp.float32)
    grad_gates = jnp.sum(upstream[:, None, :] * paired, axis=-1)
    grad_paired = (
        (gate_values[:, :, None] * upstream[:, None, :])
        .astype(jnp.bfloat16)
        .reshape(2 * tokens, -1)
    )
    grad_expert = (
        jnp.zeros((experts * capacity, grad_paired.shape[1]), jnp.bfloat16)
        .at[target]
        .set(grad_paired)
        .reshape(experts, capacity, -1)
    )
    gate_all, up_all, down_all = (
        lax.all_gather(w_gate, ("seq", "fsdp"), axis=1, tiled=True),
        lax.all_gather(w_up, ("seq", "fsdp"), axis=1, tiled=True),
        lax.all_gather(w_down, ("seq", "fsdp"), axis=1, tiled=True),
    )
    grad_hidden = jnp.einsum(
        "ecd,efd->ecf", grad_expert, down_all, preferred_element_type=jnp.float32
    )
    grad_gate_pre = (
        grad_hidden * up_pre * sigmoid_gate * (1.0 + gate_pre * (1.0 - sigmoid_gate))
    ).astype(jnp.bfloat16)
    grad_up_pre = (grad_hidden * activated).astype(jnp.bfloat16)
    shard_gates = []
    shard_ups = []
    shard_downs = []
    for expert in range(experts):
        grad_down_one = jnp.dot(
            hidden[expert].T, grad_expert[expert], preferred_element_type=jnp.float32
        )
        grad_gate_one = jnp.dot(
            packed[expert].T, grad_gate_pre[expert], preferred_element_type=jnp.float32
        )
        grad_up_one = jnp.dot(
            packed[expert].T, grad_up_pre[expert], preferred_element_type=jnp.float32
        )
        piece_gate, piece_up, piece_down = (
            lax.psum_scatter(grad_gate_one, ("seq", "fsdp"), scatter_dimension=0, tiled=True),
            lax.psum_scatter(grad_up_one, ("seq", "fsdp"), scatter_dimension=0, tiled=True),
            lax.psum_scatter(grad_down_one, ("seq", "fsdp"), scatter_dimension=0, tiled=True),
        )
        shard_gates.append(piece_gate)
        shard_ups.append(piece_up)
        shard_downs.append(piece_down)
    shard_gate = jnp.stack(shard_gates, axis=0)
    shard_up = jnp.stack(shard_ups, axis=0)
    shard_down = jnp.stack(shard_downs, axis=0)
    grad_packed = jnp.einsum(
        "ecf,edf->ecd", grad_gate_pre, gate_all, preferred_element_type=jnp.float32
    ) + jnp.einsum("ecf,edf->ecd", grad_up_pre, up_all, preferred_element_type=jnp.float32)
    grad_normed2 = jnp.sum(
        grad_packed.reshape(experts * capacity, -1)[target].reshape(tokens, 2, -1), axis=1
    )
    grad_picked = gate_values * (
        grad_gates - jnp.sum(gate_values * grad_gates, axis=-1, keepdims=True)
    )
    grad_logits = jnp.sum(choose * grad_picked[:, :, None], axis=1).astype(jnp.bfloat16)
    grad_router = jnp.dot(normed2.T, grad_logits, preferred_element_type=jnp.float32)
    grad_normed2 = grad_normed2 + jnp.dot(
        grad_logits, router_all.T, preferred_element_type=jnp.float32
    )
    grad_gain_second = jnp.sum(grad_normed2 * plain_second, axis=0)
    grad_plain2 = grad_normed2 * gain_two
    grad_mixed = (
        upstream
        + factor_second * grad_plain2
        - mixed * factor_second**3 * jnp.mean(grad_plain2 * mixed, axis=-1, keepdims=True)
    )
    grad_proj = grad_mixed.astype(jnp.bfloat16)
    grad_out = jnp.dot(attn_tokens.T, grad_proj, preferred_element_type=jnp.float32)
    grad_attn = jnp.dot(grad_proj, out_all.T, preferred_element_type=jnp.float32).astype(
        jnp.bfloat16
    )
    grad_attn_heads = lax.all_to_all(grad_attn, "seq", split_axis=1, concat_axis=0, tiled=True)
    grad_query_heads, grad_key_heads, grad_value_heads = attention_backward(
        query_heads,
        key_heads,
        value_heads,
        grad_attn_heads.reshape(query_heads.shape),
        log_totals,
        block_rows,
        score_scale,
    )
    grad_queries, grad_keys, grad_values = (
        lax.all_to_all(grad_query_heads, "seq", split_axis=0, concat_axis=1, tiled=True),
        lax.all_to_all(grad_key_heads, "seq", split_axis=0, concat_axis=1, tiled=True),
        lax.all_to_all(grad_value_heads, "seq", split_axis=0, concat_axis=1, tiled=True),
    )
    grad_query = jnp.dot(normed1.T, grad_queries, preferred_element_type=jnp.float32)
    grad_key = jnp.dot(normed1.T, grad_keys, preferred_element_type=jnp.float32)
    grad_value = jnp.dot(normed1.T, grad_values, preferred_element_type=jnp.float32)
    grad_normed1 = (
        jnp.dot(grad_queries, query_all.T, preferred_element_type=jnp.float32)
        + jnp.dot(grad_keys, key_all.T, preferred_element_type=jnp.float32)
        + jnp.dot(grad_values, value_all.T, preferred_element_type=jnp.float32)
    )
    grad_gain_first = jnp.sum(grad_normed1 * plain_first, axis=0)
    grad_plain1 = grad_normed1 * gain_one
    grad_inputs = (
        grad_mixed
        + factor_first * grad_plain1
        - inputs * factor_first**3 * jnp.mean(grad_plain1 * inputs, axis=-1, keepdims=True)
    )
    (
        shard_gain_first,
        shard_query,
        shard_key,
        shard_value,
        shard_out,
        shard_gain_second,
        shard_router,
    ) = (
        lax.psum_scatter(grad_gain_first, ("seq", "fsdp"), scatter_dimension=0, tiled=True),
        lax.psum_scatter(grad_query, ("seq", "fsdp"), scatter_dimension=0, tiled=True),
        lax.psum_scatter(grad_key, ("seq", "fsdp"), scatter_dimension=0, tiled=True),
        lax.psum_scatter(grad_value, ("seq", "fsdp"), scatter_dimension=0, tiled=True),
        lax.psum_scatter(grad_out, ("seq", "fsdp"), scatter_dimension=0, tiled=True),
        lax.psum_scatter(grad_gain_second, ("seq", "fsdp"), scatter_dimension=0, tiled=True),
        lax.psum_scatter(grad_router, ("seq", "fsdp"), scatter_dimension=0, tiled=True),
    )
    return (
        output,
        grad_inputs.astype(jnp.bfloat16)[None],
        shard_gain_first,
        shard_query,
        shard_key,
        shard_value,
        shard_out,
        shard_gain_second,
        shard_router,
        shard_gate,
        shard_up,
        shard_down,
    )


def solution(mesh):
    placed = (
        P("fsdp", "seq", None),
        P("fsdp", "seq", None),
        P("fsdp", "seq", None),
        P(("seq", "fsdp")),
        P(("seq", "fsdp"), None),
        P(("seq", "fsdp"), None),
        P(("seq", "fsdp"), None),
        P(("seq", "fsdp"), None),
        P(("seq", "fsdp")),
        P(("seq", "fsdp"), None),
        P(None, ("seq", "fsdp"), None),
        P(None, ("seq", "fsdp"), None),
        P(None, ("seq", "fsdp"), None),
    )
    return jax.shard_map(
        shards,
        mesh=mesh,
        in_specs=placed,
        out_specs=(
            P("fsdp", "seq", None),
            P("fsdp", "seq", None),
            P(("seq", "fsdp")),
            P(("seq", "fsdp"), None),
            P(("seq", "fsdp"), None),
            P(("seq", "fsdp"), None),
            P(("seq", "fsdp"), None),
            P(("seq", "fsdp")),
            P(("seq", "fsdp"), None),
            P(None, ("seq", "fsdp"), None),
            P(None, ("seq", "fsdp"), None),
            P(None, ("seq", "fsdp"), None),
        ),
        check_vma=False,
    )
```

profile of v0, /device:TPU:0, one launch (start us, length us, event | category | flops | bytes accessed | tf_op | source)
XLA Modules:
  0.0 2632.8 jit_solution(10918352400219750068)
XLA Ops:
  14.7 42.2 %all-reduce.5 = (bf16[1536]{0:T(1024)(128)(2,1)S(1)}, bf16[1536]{0:T(1024)(128)(2,1)S(1)}) all-reduce(bf16[1536]{0:T(1024)(128)(2,1)S(1)} %dynamic-update-slice, bf16[1536]{0:T(1024)(128)(2,1)S(1)} %dynamic-update-slice.1), channel_id=1, replica_groups=mesh['seq'=4,'fsdp'=8] {'seq','fsdp'}, use_global_device_ids=true, to_apply=%add | all-reduce | flops 3072 | bytes 12288
  60.5 8.4 all-gather.11.cloned.1.call-done
  75.1 50.9 %all-gather.13.cloned.1.call-done = bf16[1536,512]{1,0:T(8,128)(2,1)} async-done(((bf16[48,512]{1,0:T(8,128)(2,1)}), bf16[1536,512]{1,0:T(8,128)(2,1)}) %all-gather.13.cloned.1.call-update) | async-done | bytes 1572880 | tf_op jit(solution)/shard_map/all_gather | solution.py:116
  132.1 59.4 %all-gather.9.cloned.1.call-done = bf16[1536,1536]{1,0:T(8,128)(2,1)} async-done(((bf16[48,1536]{1,0:T(8,128)(2,1)}), bf16[1536,1536]{1,0:T(8,128)(2,1)}) %all-gather.9.cloned.1.call-update) | async-done | bytes 4718608 | tf_op jit(solution)/shard_map/all_gather | solution.py:114
  208.0 5.4 all-to-all-done
  220.0 25.7 while.27
  261.0 5.2 mul.273
  266.3 40.9 %all-gather = bf16[32,48,4]{1,2,0:T(4,128)(2,1)S(1)} all-gather(bf16[1,48,4]{1,2,0:T(4,128)(2,1)S(1)} %bitcast.424), channel_id=1, replica_groups=mesh['seq'=4,'fsdp'=8] {'seq','fsdp'}, dimensions={0}, use_global_device_ids=true | all-gather | bytes 12672 | tf_op jit(solution)/shard_map/all_gather | solution.py:119
  319.0 6.4 scatter_custom_fusion.1
  325.5 32.6 %all-gather.17.cloned.1.call-done = bf16[4,1536,1024]{2,1,0:T(8,128)(2,1)} async-done(((bf16[4,48,1024]{2,1,0:T(8,128)(2,1)}), bf16[4,1536,1024]{2,1,0:T(8,128)(2,1)}) %all-gather.17.cloned.1.call-update) | async-done | bytes 12582928 | tf_op jit(solution)/shard_map/all_gather | solution.py:122
  358.1 8.8 fusion.128
  366.9 88.4 %all-gather.19.cloned.1.call-done = bf16[4,1536,1024]{2,1,0:T(8,128)(2,1)} async-done(((bf16[4,48,1024]{2,1,0:T(8,128)(2,1)}), bf16[4,1536,1024]{2,1,0:T(8,128)(2,1)}) %all-gather.19.cloned.1.call-update) | async-done | bytes 12582928 | tf_op jit(solution)/shard_map/all_gather | solution.py:123
  455.3 8.9 fusion.129
  464.1 88.4 %all-gather.21.cloned.1.call-done = bf16[4,1024,1536]{2,1,0:T(8,128)(2,1)} async-done(((bf16[4,32,1536]{2,1,0:T(8,128)(2,1)}), bf16[4,1024,1536]{2,1,0:T(8,128)(2,1)}) %all-gather.21.cloned.1.call-update) | async-done | bytes 12582928 | tf_op jit(solution)/shard_map/all_gather | solution.py:124
  552.6 13.8 multiply_convert_fusion
  566.3 9.8 fusion.130
  576.2 7.0 gather_fusion.1
  583.2 5.0 reshape.380
  588.3 9.2 multiply_reduce_fusion
  599.0 4.7 fusion.87
  603.8 4.6 fusion.91
  608.5 4.6 fusion.95
  613.2 4.6 fusion.99
  617.9 4.7 fusion.85
  622.7 4.6 fusion.89
  627.5 4.6 fusion.93
  632.4 4.7 fusion.97
  638.4 4.7 fusion.77
  643.2 4.6 fusion.79
  647.9 4.9 fusion.81
  652.8 7.9 fusion.131
  660.8 11.1 convolution_add_fusion
  671.8 6.0 gather_fusion.2
  681.3 5.7 reduce_sum.153
  699.7 4.8 fusion.83
  704.6 6.5 all-to-all-done.4
  714.2 57.6 %while.28 = (s32[]{:T(128)}, f32[1024,2,64]{0,2,1:T(8,128)S(1)}, f32[1024,2,64]{0,2,1:T(8,128)}, bf16[2,512,2,3,64]{1,4,3,2,0:T(8,128)(2,1)}, bf16[2,512,2,3,64]...) while((s32[]{:T(128)}, f32[1024,2,64]{0,2,1:T(8,128)S(1)}, ...), condition=%wide.region_22.23_spmd.clone, body=%wide.region_20.22_spmd.clone.sunk | while | flops 2062022144 | bytes 184250800 | solution.py:87
  718.0 5.7 fusion.199
  723.8 5.0 fusion.200
  733.3 6.9 fusion.202
  746.8 5.7 fusion.199
  752.5 5.0 fusion.200
  761.8 7.0 fusion.202
  772.0 9.7 all_to_all.134
  785.5 8.2 all_to_all.135
  798.4 5.1 fusion.101
  809.1 10.9 all_to_all.136
  820.0 5.2 fusion.122
  834.4 37.7 %all-reduce.4 = (f32[1536]{0:T(1024)S(1)}, f32[1536]{0:T(1024)S(1)}) all-reduce(f32[1536]{0:T(1024)S(1)} %get-tuple-element.248, f32[1536]{0:T(1024)S(1)} %copy-done.39), channel_id=2, replica_groups=mesh['seq'=4,'fsdp'=8] {'seq','fsdp'}, use_global_device_ids=true, to_apply=%region_25.26.clone | all-reduce | flops 3072 | bytes 24576
  875.9 56.7 %reduce-scatter.32.cloned.1.call-done = f32[48,1024]{1,0:T(8,128)} async-done(((f32[1536,1024]{1,0:T(8,128)}), f32[48,1024]{1,0:T(8,128)}) %reduce-scatter.32.cloned.1.call-update) | async-done | bytes 196624 | tf_op jit(solution)/shard_map/reduce_scatter | solution.py:222
  932.6 119.5 %reduce-scatter.30.cloned.1.call-done = f32[48,1024]{1,0:T(8,128)} async-done(((f32[1536,1024]{1,0:T(8,128)}), f32[48,1024]{1,0:T(8,128)}) %reduce-scatter.30.cloned.1.call-update) | async-done | bytes 196624 | tf_op jit(solution)/shard_map/reduce_scatter | solution.py:222
  1052.1 120.0 %reduce-scatter.28.cloned.1.call-done = f32[48,1024]{1,0:T(8,128)} async-done(((f32[1536,1024]{1,0:T(8,128)}), f32[48,1024]{1,0:T(8,128)}) %reduce-scatter.28.cloned.1.call-update) | async-done | bytes 196624 | tf_op jit(solution)/shard_map/reduce_scatter | solution.py:222
  1174.2 117.2 %reduce-scatter.42.cloned.1.call-done = f32[48,1024]{1,0:T(8,128)} async-done(((f32[1536,1024]{1,0:T(8,128)}), f32[48,1024]{1,0:T(8,128)}) %reduce-scatter.42.cloned.1.call-update) | async-done | bytes 196624 | tf_op jit(solution)/shard_map/reduce_scatter | solution.py:223
  1291.5 120.0 %reduce-scatter.40.cloned.1.call-done = f32[48,1024]{1,0:T(8,128)} async-done(((f32[1536,1024]{1,0:T(8,128)}), f32[48,1024]{1,0:T(8,128)}) %reduce-scatter.40.cloned.1.call-update) | async-done | bytes 196624 | tf_op jit(solution)/shard_map/reduce_scatter | solution.py:223
  1411.5 119.3 %reduce-scatter.38.cloned.1.call-done = f32[48,1024]{1,0:T(8,128)} async-done(((f32[1536,1024]{1,0:T(8,128)}), f32[48,1024]{1,0:T(8,128)}) %reduce-scatter.38.cloned.1.call-update) | async-done | bytes 196624 | tf_op jit(solution)/shard_map/reduce_scatter | solution.py:223
  1530.7 120.2 %reduce-scatter.36.cloned.1.call-done = f32[48,1024]{1,0:T(8,128)} async-done(((f32[1536,1024]{1,0:T(8,128)}), f32[48,1024]{1,0:T(8,128)}) %reduce-scatter.36.cloned.1.call-update) | async-done | bytes 196624 | tf_op jit(solution)/shard_map/reduce_scatter | solution.py:223
  1653.1 117.1 %reduce-scatter.50.cloned.1.call-done = f32[32,1536]{1,0:T(8,128)} async-done(((f32[1024,1536]{1,0:T(8,128)}), f32[32,1536]{1,0:T(8,128)}) %reduce-scatter.50.cloned.1.call-update) | async-done | bytes 196624 | tf_op jit(solution)/shard_map/reduce_scatter | solution.py:224
  1770.3 120.2 %reduce-scatter.48.cloned.1.call-done = f32[32,1536]{1,0:T(8,128)} async-done(((f32[1024,1536]{1,0:T(8,128)}), f32[32,1536]{1,0:T(8,128)}) %reduce-scatter.48.cloned.1.call-update) | async-done | bytes 196624 | tf_op jit(solution)/shard_map/reduce_scatter | solution.py:224
  1890.5 119.1 %reduce-scatter.46.cloned.1.call-done = f32[32,1536]{1,0:T(8,128)} async-done(((f32[1024,1536]{1,0:T(8,128)}), f32[32,1536]{1,0:T(8,128)}) %reduce-scatter.46.cloned.1.call-update) | async-done | bytes 196624 | tf_op jit(solution)/shard_map/reduce_scatter | solution.py:224
  2009.7 119.9 %reduce-scatter.44.cloned.1.call-done = f32[32,1536]{1,0:T(8,128)} async-done(((f32[1024,1536]{1,0:T(8,128)}), f32[32,1536]{1,0:T(8,128)}) %reduce-scatter.44.cloned.1.call-update) | async-done | bytes 196624 | tf_op jit(solution)/shard_map/reduce_scatter | solution.py:224
  2131.7 104.6 %reduce-scatter.22.cloned.1.call-done = f32[48,512]{1,0:T(8,128)} async-done(((f32[1536,512]{1,0:T(8,128)}), f32[48,512]{1,0:T(8,128)}) %reduce-scatter.22.cloned.1.call-update) | async-done | bytes 98320 | tf_op jit(solution)/shard_map/reduce_scatter | solution.py:299
  2236.4 106.4 %reduce-scatter.24.cloned.1.call-done = f32[48,512]{1,0:T(8,128)} async-done(((f32[1536,512]{1,0:T(8,128)}), f32[48,512]{1,0:T(8,128)}) %reduce-scatter.24.cloned.1.call-update) | async-done | bytes 98320 | tf_op jit(solution)/shard_map/reduce_scatter | solution.py:300
  2342.8 141.0 %reduce-scatter.26.cloned.1.call-done = f32[48,1536]{1,0:T(8,128)} async-done(((f32[1536,1536]{1,0:T(8,128)}), f32[48,1536]{1,0:T(8,128)}) %reduce-scatter.26.cloned.1.call-update) | async-done | bytes 294928 | tf_op jit(solution)/shard_map/reduce_scatter | solution.py:301
  2483.8 141.9 %reduce-scatter.20.cloned.1.call-done = f32[48,1536]{1,0:T(8,128)} async-done(((f32[1536,1536]{1,0:T(8,128)}), f32[48,1536]{1,0:T(8,128)}) %reduce-scatter.20.cloned.1.call-update) | async-done | bytes 294928 | tf_op jit(solution)/shard_map/reduce_scatter | solution.py:298
  (304 shorter events, 176.8 us)
Async XLA Ops:
  7.2 52.5 %copy-start.5 = (bf16[1,256,1536]{2,1,0:T(8,128)(2,1)S(1)}, bf16[1,256,1536]{2,1,0:T(8,128)(2,1)}, u32[]{:S(2)}) copy-start(bf16[1,256,1536]{2,1,0:T(8,128)(2,1)} %param.17) | copy-start | bytes 2359300
  7.2 61.7 %all-gather.11.cloned.1.call-start = ((), (), s32[]{:S(2)}) async-start(), calls=%async_computation.26 | async-start | bytes 1622016 | tf_op jit(solution)/shard_map/all_gather | solution.py:115
  7.9 118.0 %all-gather.13.cloned.1.call-start = ((), (), s32[]{:S(2)}) async-start(), calls=%async_computation.27 | async-start | bytes 1622016 | tf_op jit(solution)/shard_map/all_gather | solution.py:116
  8.7 182.9 %all-gather.9.cloned.1.call-start = ((), (), s32[]{:S(2)}) async-start(), calls=%async_computation.25 | async-start | bytes 4866048 | tf_op jit(solution)/shard_map/all_gather | solution.py:114
  9.4 300.5 %all-gather.15.cloned.1.call-start = ((), (), s32[]{:S(2)}) async-start(), calls=%async_computation.28 | async-start | bytes 4866048 | tf_op jit(solution)/shard_map/all_gather | solution.py:117
  10.0 348.1 %all-gather.17.cloned.1.call-start = ((), (), s32[]{:S(2)}) async-start(), calls=%async_computation.29 | async-start | bytes 12976128 | tf_op jit(solution)/shard_map/all_gather | solution.py:122
  10.6 444.7 %all-gather.19.cloned.1.call-start = ((), (), s32[]{:S(2)}) async-start(), calls=%async_computation.30 | async-start | bytes 12976128 | tf_op jit(solution)/shard_map/all_gather | solution.py:123
  11.1 541.4 %all-gather.21.cloned.1.call-start = ((), (), s32[]{:S(2)}) async-start(), calls=%async_computation.31 | async-start | bytes 12976128 | tf_op jit(solution)/shard_map/all_gather | solution.py:124
  57.0 134.6 %copy-start.33 = (f32[1536]{0:T(1024)}, f32[1536]{0:T(1024)S(1)}, u32[]{:S(2)}) copy-start(f32[1536]{0:T(1024)S(1)} %convert_element_type.122) | copy-start | bytes 18436
  60.5 131.1 %copy-start.37 = (f32[256]{0:T(256)}, f32[256]{0:T(256)S(1)}, u32[]{:S(2)}) copy-start(f32[256]{0:T(256)S(1)} %get-tuple-element.298) | copy-start | bytes 3076
  71.7 57.1 %all-to-all-start.1 = ((bf16[256,4,128]{2,0,1:T(8,128)(2,1)}), bf16[256,4,128]{2,0,1:T(8,128)(2,1)S(1)}, u32[]{:S(2)}, u32[]{:S(2)}) async-start(bf16[256,4,128]{2,0,1:T(8,128)(2,1)} %bitcast.326), calls=%async_computation.1 | async-start | bytes 524288 | tf_op jit(solution)/shard_map/all_to_all | solution.py:137
  128.7 67.8 %all-to-all-start.2 = ((bf16[256,4,128]{2,0,1:T(8,128)(2,1)}), bf16[256,4,128]{2,0,1:T(8,128)(2,1)S(1)}, u32[]{:S(2)}, u32[]{:S(2)}) async-start(bf16[256,4,128]{2,0,1:T(8,128)(2,1)} %bitcast.325), calls=%async_computation.2 | async-start | bytes 524288 | tf_op jit(solution)/shard_map/all_to_all | solution.py:138
  197.2 16.2 all-to-all-start
  202.2 56.0 %copy-start.9 = (f32[256,1536]{1,0:T(8,128)}, f32[256,1536]{1,0:T(8,128)S(1)}, u32[]{:S(2)}) copy-start(f32[256,1536]{1,0:T(8,128)S(1)} %bitcast_convert_fusion) | copy-start | bytes 4718596
  223.9 3.6 copy-start.17
  223.9 3.6 copy-start.22
  236.8 3.6 copy-start.17
  236.8 3.6 copy-start.22
  245.7 8.7 copy-start.1
  245.7 8.7 copy-start.3
  245.7 8.7 copy-start.35
  245.7 8.7 copy-start.43
  254.4 55.4 %all-to-all-start.3 = ((bf16[4,256,384]{1,2,0:T(8,128)(2,1)}), bf16[4,256,384]{1,2,0:T(8,128)(2,1)S(1)}, u32[]{:S(2)}, u32[]{:S(2)}) async-start(bf16[4,256,384]{1,2,0:T(8,128)(2,1)} %copy.144), calls=%async_computation.3 | async-start | bytes 1572864 | tf_op jit(solution)/shard_map/all_to_all | solution.py:151
  258.0 567.3 %reduce-scatter.52.cloned.1.call-start = ((), (), s32[]{:S(2)}) async-start(), calls=%async_computation.48 | async-start | bytes 811008
  261.0 5.3 copy-start.42
  309.9 4.1 copy-start.12
  315.4 3.2 copy-start.40
  599.0 276.9 %reduce-scatter.34.cloned.1.call-start = ((), (), s32[]{:S(2)}) async-start(), calls=%async_computation.39 | async-start | bytes 6488064 | tf_op jit(solution)/shard_map/reduce_scatter | solution.py:222
  603.8 328.8 %reduce-scatter.32.cloned.1.call-start = ((), (), s32[]{:S(2)}) async-start(), calls=%async_computation.38 | async-start | bytes 6488064 | tf_op jit(solution)/shard_map/reduce_scatter | solution.py:222
  608.5 443.6 %reduce-scatter.30.cloned.1.call-start = ((), (), s32[]{:S(2)}) async-start(), calls=%async_computation.37 | async-start | bytes 6488064 | tf_op jit(solution)/shard_map/reduce_scatter | solution.py:222
  613.2 558.9 %reduce-scatter.28.cloned.1.call-start = ((), (), s32[]{:S(2)}) async-start(), calls=%async_computation.36 | async-start | bytes 6488064 | tf_op jit(solution)/shard_map/reduce_scatter | solution.py:222
  617.9 673.6 %reduce-scatter.42.cloned.1.call-start = ((), (), s32[]{:S(2)}) async-start(), calls=%async_computation.43 | async-start | bytes 6488064 | tf_op jit(solution)/shard_map/reduce_scatter | solution.py:223
  622.7 788.8 %reduce-scatter.40.cloned.1.call-start = ((), (), s32[]{:S(2)}) async-start(), calls=%async_computation.42 | async-start | bytes 6488064 | tf_op jit(solution)/shard_map/reduce_scatter | solution.py:223
  627.4 903.3 %reduce-scatter.38.cloned.1.call-start = ((), (), s32[]{:S(2)}) async-start(), calls=%async_computation.41 | async-start | bytes 6488064 | tf_op jit(solution)/shard_map/reduce_scatter | solution.py:223
  632.1 1018.8 %reduce-scatter.36.cloned.1.call-start = ((), (), s32[]{:S(2)}) async-start(), calls=%async_computation.40 | async-start | bytes 6488064 | tf_op jit(solution)/shard_map/reduce_scatter | solution.py:223
  637.0 1133.2 %reduce-scatter.50.cloned.1.call-start = ((), (), s32[]{:S(2)}) async-start(), calls=%async_computation.47 | async-start | bytes 6488064 | tf_op jit(solution)/shard_map/reduce_scatter | solution.py:224
  643.2 1247.3 %reduce-scatter.48.cloned.1.call-start = ((), (), s32[]{:S(2)}) async-start(), calls=%async_computation.46 | async-start | bytes 6488064 | tf_op jit(solution)/shard_map/reduce_scatter | solution.py:224
  647.9 1361.8 %reduce-scatter.46.cloned.1.call-start = ((), (), s32[]{:S(2)}) async-start(), calls=%async_computation.45 | async-start | bytes 6488064 | tf_op jit(solution)/shard_map/reduce_scatter | solution.py:224
  652.8 7.9 copy-start.15
  681.3 5.7 copy-start.8
  696.1 15.0 all-to-all-start.4
  699.6 1430.0 %reduce-scatter.44.cloned.1.call-start = ((), (), s32[]{:S(2)}) async-start(), calls=%async_computation.44 | async-start | bytes 6488064 | tf_op jit(solution)/shard_map/reduce_scatter | solution.py:224
  704.5 1531.8 %reduce-scatter.22.cloned.1.call-start = ((), (), s32[]{:S(2)}) async-start(), calls=%async_computation.33 | async-start | bytes 3244032 | tf_op jit(solution)/shard_map/reduce_scatter | solution.py:299
  711.7 2.5 copy-start.2
  716.2 7.5 copy-start
  728.8 4.4 copy-start.16
  728.8 4.4 copy-start.30
  728.8 11.4 slice-start
  733.2 7.0 slice-start.1
  733.2 7.0 copy-start.19
  745.0 7.5 copy-start
  757.6 4.2 copy-start.16
  757.6 4.2 copy-start.30
  757.6 11.2 slice-start
  761.8 7.0 slice-start.1
  761.8 7.0 copy-start.19
  771.8 10.0 copy-start.6
  771.8 10.0 copy-start.34
  771.8 10.0 copy-start.38
  784.2 1558.6 %reduce-scatter.24.cloned.1.call-start = ((), (), s32[]{:S(2)}) async-start(), calls=%async_computation.34 | async-start | bytes 3244032 | tf_op jit(solution)/shard_map/reduce_scatter | solution.py:300
  796.8 1687.0 %reduce-scatter.26.cloned.1.call-start = ((), (), s32[]{:S(2)}) async-start(), calls=%async_computation.35 | async-start | bytes 9732096 | tf_op jit(solution)/shard_map/reduce_scatter | solution.py:301
  803.5 1822.2 %reduce-scatter.20.cloned.1.call-start = ((), (), s32[]{:S(2)}) async-start(), calls=%async_computation.32 | async-start | bytes 9732096 | tf_op jit(solution)/shard_map/reduce_scatter | solution.py:298
  826.7 4.1 copy-start.27
  832.3 40.9 %copy-start.41 = (f32[256]{0:T(256)S(1)}, f32[256]{0:T(256)}, u32[]{:S(2)}) copy-start(f32[256]{0:T(256)} %get-tuple-element.297) | copy-start | bytes 3076
  (23 other events, 33.0 us)
Sparse Core Ops, SparseCore 0:
  11.0 57.7 all-gather.10
  71.9 54.0 all-gather.12
  129.0 62.5 all-gather.8
  194.4 65.6 all-gather.14
  263.0 95.0 all-gather.16
  361.0 94.2 all-gather.18
  458.3 94.2 all-gather.20
  599.1 93.6 reduce-scatter.51
  698.5 113.3 reduce-scatter.33
  818.3 114.2 reduce-scatter.31
  938.2 113.8 reduce-scatter.29
  1058.5 113.4 reduce-scatter.27
  1177.7 113.7 reduce-scatter.41
  1297.9 113.5 reduce-scatter.39
  1417.0 113.7 reduce-scatter.37
  1537.2 113.7 reduce-scatter.35
  1656.4 113.7 reduce-scatter.49
  1776.7 113.7 reduce-scatter.47
  1896.1 113.4 reduce-scatter.45
  2016.1 113.4 reduce-scatter.43
  2135.6 100.7 reduce-scatter.21
  2242.4 100.4 reduce-scatter.23
  2349.3 134.5 reduce-scatter.25
  2491.2 134.4 reduce-scatter.19
where the time goes:
time: 2640 us; the launch traced here: 2630 us
  waiting for transfers between devices  2090 us (79%)
  matrix products  212 us (8%)
  blocking collectives  150 us (6%)
  local copies, waits for them, and re-layouts  89.9 us (3%)
  other arithmetic  58.3 us (2%)
    reduce_scatter x4, waiting for transfers between devices, shards(): lax.psum_scatter(grad_up_one, ('seq', 'fsdp'), scatter_dimension=0, tiled...  477 us
    reduce_scatter x4, waiting for transfers between devices, shards(): lax.psum_scatter(grad_down_one, ('seq', 'fsdp'), scatter_dimension=0, til...  476 us
    reduce_scatter x4, waiting for transfers between devices, shards(): lax.psum_scatter(grad_gate_one, ('seq', 'fsdp'), scatter_dimension=0, til...  296 us
    reduce_scatter x1, waiting for transfers between devices, shards(): lax.psum_scatter(grad_query, ('seq', 'fsdp'), scatter_dimension=0, tiled=...  142 us
    reduce_scatter x1, waiting for transfers between devices, shards(): lax.psum_scatter(grad_out, ('seq', 'fsdp'), scatter_dimension=0, tiled=True)  141 us
    reduce_scatter x1, waiting for transfers between devices, shards(): lax.psum_scatter(grad_value, ('seq', 'fsdp'), scatter_dimension=0, tiled=...  106 us
    reduce_scatter x1, waiting for transfers between devices, shards(): lax.psum_scatter(grad_key, ('seq', 'fsdp'), scatter_dimension=0, tiled=True)  105 us
    all_gather x1, waiting for transfers between devices, shards(): lax.all_gather(w_down, ('seq', 'fsdp'), axis=1, tiled=True)  88.4 us
  transfers between devices with their start and end apart: 29, of which 23 were waited for; matrix products, arithmetic and copies ran while one was open for 11% of the time, Pallas kernels for 0%

commit v1 on v0

v1 whole, which is shorter than its diff:
```python
import jax
import jax.numpy as jnp
from jax import lax
from jax.sharding import PartitionSpec as P

HEADS = 24
KV_HEADS = 8
HEAD_DIM = 64
EPS = 1e-06
SCALE = HEAD_DIM ** (-0.5)
BF = jnp.bfloat16
F32 = jnp.float32


def dot(a, b):
    return jnp.dot(a, b, preferred_element_type=F32)


def dot_t(a, b):
    return lax.dot_general(a, b, (((1,), (1,)), ((), ())), preferred_element_type=F32)


def t_dot(a, b):
    return lax.dot_general(a, b, (((0,), (0,)), ((), ())), preferred_element_type=F32)


def rms_factor(rows):
    return lax.rsqrt(jnp.mean(rows * rows, axis=-1, keepdims=True) + EPS)


def scores_of(q, k):
    length = q.shape[0]
    sc = SCALE * jnp.einsum("qgrd,kgd->grqk", q, k, preferred_element_type=F32)
    pos = jnp.arange(length)
    return jnp.where(pos[None, :] <= pos[:, None], sc, -1e30)


def shards(x, cot, routes, gain_attn, w_query, w_key, w_value, w_out, gain_ffn, router, w_gate, w_up, w_down):
    n_seq = lax.axis_size("seq")
    n_fsdp = lax.axis_size("fsdp")
    rows, d = w_query.shape
    experts, ff_rows, _ = w_down.shape
    ff = w_gate.shape[2]
    fc = ff // n_seq
    toks = x.shape[1]

    extra = jnp.concatenate(
        [gain_attn[:, None], gain_ffn[:, None], router, jnp.zeros((rows, 128 - 2 - experts), BF)], axis=1
    )
    qkv = jnp.concatenate(
        [w_query.reshape(rows, n_seq, -1), w_key.reshape(rows, n_seq, -1), w_value.reshape(rows, n_seq, -1),
         jnp.broadcast_to(extra[:, None], (rows, n_seq, 128))], axis=2,
    )
    gu = jnp.stack([w_gate, w_up]).reshape(2, experts, rows, n_seq, fc).transpose(3, 2, 0, 1, 4)
    gu = gu.reshape(n_seq, rows, 2 * experts * fc)
    qkv = qkv.transpose(1, 0, 2)
    qkv = lax.all_to_all(qkv, "seq", split_axis=0, concat_axis=0, tiled=True)
    gu = lax.all_to_all(gu, "seq", split_axis=0, concat_axis=0, tiled=True)
    do = jnp.concatenate([w_down.reshape(experts * ff_rows, d), w_out], axis=0)
    qkv = lax.all_gather(qkv, "fsdp", axis=1).reshape(d, -1)
    do = lax.all_gather(do, "fsdp", axis=0)
    wo = do[:, experts * ff_rows:].reshape(-1, d)
    wd = do[:, : experts * ff_rows].reshape(n_fsdp, experts, ff_rows, d).transpose(1, 0, 2, 3).reshape(-1, d)
    gu = lax.all_gather(gu, "fsdp", axis=1).reshape(d, -1)

    nq, nk = w_query.shape[1] // n_seq, w_key.shape[1] // n_seq
    nqkv = nq + 2 * nk
    gain_one = qkv[:, nqkv].astype(F32)
    gain_two = qkv[:, nqkv + 1].astype(F32)
    wr = qkv[:, nqkv + 2: nqkv + 2 + experts]
    wqkv = qkv[:, :nqkv]

    xs = lax.all_gather(x[0], "seq", axis=0, tiled=True)
    gs = lax.all_gather(cot[0], "seq", axis=0, tiled=True)
    ids = lax.all_gather(routes[0], "seq", axis=0, tiled=True)
    xf = xs.astype(F32)
    n1 = (xf * rms_factor(xf) * gain_one).astype(BF)
    length = xs.shape[0]
    proj = dot(n1, wqkv).astype(BF)
    q = proj[:, :nq].reshape(length, nk // HEAD_DIM, -1, HEAD_DIM)
    k = proj[:, nq: nq + nk].reshape(length, -1, HEAD_DIM)
    v = proj[:, nq + nk:].reshape(length, -1, HEAD_DIM)
    sc = scores_of(q, k)
    m = jnp.max(sc, axis=-1, keepdims=True)
    e = jnp.exp(sc - m)
    tot = jnp.sum(e, axis=-1, keepdims=True)
    prob = (e / tot).astype(BF)
    lse = m + jnp.log(tot)
    attn = jnp.einsum("grqk,kgd->qgrd", prob, v, preferred_element_type=F32).astype(BF).reshape(length, nq)
    part = dot(attn, wo).astype(BF)
    mine = lax.psum_scatter(part, "seq", scatter_dimension=0, tiled=True)
    xo = x[0].astype(F32)
    mixed = xo + mine.astype(F32)
    r2 = rms_factor(mixed)
    n2o = (mixed * r2 * gain_two).astype(BF)

    n2 = lax.all_gather(n2o, "seq", axis=0, tiled=True)
    logits = dot(n2, wr)
    hot = ids[:, :, None] == jnp.arange(experts)[None, None, :]
    named = jnp.any(hot, axis=1)
    lm = jnp.max(jnp.where(named, logits, -1e30), axis=-1, keepdims=True)
    le = jnp.where(named, jnp.exp(logits - lm), 0.0)
    gates = le / jnp.sum(le, axis=-1, keepdims=True)
    pre = dot(n2, gu)
    gp, up = pre[:, : experts * fc], pre[:, experts * fc:]
    dh0 = dot_t(gs, wd)
    sig = jax.nn.sigmoid(gp)
    act = gp * sig
    hid = (act * up).astype(BF).astype(F32)
    gw = jnp.repeat(gates, fc, axis=1)
    hg = (gw * hid).astype(BF)
    dgate = jnp.sum((hid * dh0).reshape(length, experts, fc), axis=-1)
    dh = gw * dh0
    dgp = (dh * up * sig * (1.0 + gp * (1.0 - sig))).astype(BF)
    dup = (dh * act).astype(BF)
    dpre = jnp.concatenate([dgp, dup], axis=1)
    outp = dot(hg, wd).astype(BF)
    dn2p = dot_t(dpre, gu).astype(BF)
    ggu = t_dot(n2, dpre).astype(BF)
    gwd = t_dot(hg, gs).astype(BF)
    gwd = gwd.reshape(experts, n_fsdp, ff_rows, d).transpose(1, 0, 2, 3).reshape(-1, d)
    gwd = lax.psum_scatter(gwd, "fsdp", scatter_dimension=0, tiled=True)
    ggu = ggu.reshape(n_seq, n_fsdp, rows, -1).transpose(1, 0, 2, 3).reshape(n_fsdp * n_seq * rows, -1)
    ggu = lax.psum_scatter(ggu, "fsdp", scatter_dimension=0, tiled=True).reshape(n_seq, rows, -1)
    ggu = lax.all_to_all(ggu, "seq", split_axis=0, concat_axis=0, tiled=True)

    out = lax.psum_scatter(outp, "seq", scatter_dimension=0, tiled=True)
    output = (mixed + out.astype(F32)).astype(BF)
    dn2 = lax.psum_scatter(dn2p, "seq", scatter_dimension=0, tiled=True).astype(F32)
    dgate = lax.psum_scatter(dgate, "seq", scatter_dimension=0, tiled=True)
    go = lax.dynamic_slice_in_dim(gates, lax.axis_index("seq") * toks, toks, 0)
    dlog = (go * (dgate - jnp.sum(go * dgate, axis=-1, keepdims=True))).astype(BF)
    grouter = t_dot(n2o, dlog)
    dn2 = dn2 + dot_t(dlog, wr)
    up_g = cot[0].astype(F32)
    dn = dn2 * gain_two
    dmixed = up_g + r2 * dn - mixed * r2**3 * jnp.mean(dn * mixed, axis=-1, keepdims=True)
    dprojo = dmixed.astype(BF)

    dproj = lax.all_gather(dprojo, "seq", axis=0, tiled=True)
    gwo = t_dot(attn, dproj).astype(BF)
    gwo = lax.psum_scatter(gwo, "fsdp", scatter_dimension=0, tiled=True)
    dattn = dot_t(dproj, wo).astype(BF).reshape(q.shape)
    prob = jnp.exp(scores_of(q, k) - lse)
    dprob = jnp.einsum("qgrd,kgd->grqk", dattn, v, preferred_element_type=F32)
    delta = jnp.sum(prob * dprob, axis=-1, keepdims=True)
    dsc = (prob * (dprob - delta)).astype(BF)
    dq = SCALE * jnp.einsum("grqk,kgd->qgrd", dsc, k, preferred_element_type=F32)
    dk = SCALE * jnp.einsum("grqk,qgrd->kgd", dsc, q, preferred_element_type=F32)
    dv = jnp.einsum("grqk,qgrd->kgd", prob.astype(BF), dattn, preferred_element_type=F32)
    dqkv = jnp.concatenate(
        [dq.astype(BF).reshape(length, -1), dk.astype(BF).reshape(length, -1), dv.astype(BF).reshape(length, -1)], axis=1
    )
    dn1p = dot_t(dqkv, wqkv).astype(BF)
    gqkv = t_dot(n1, dqkv).astype(BF)
    ghi = grouter.astype(BF)
    glo = (grouter - ghi.astype(F32)).astype(BF)
    gqkv = jnp.concatenate([gqkv, ghi, glo, jnp.zeros((d, 128 - 2 * experts), BF)], axis=1)
    gqkv = gqkv.reshape(n_seq, n_fsdp, rows, -1).transpose(1, 0, 2, 3).reshape(n_fsdp * n_seq * rows, -1)
    gqkv = lax.psum_scatter(gqkv, "fsdp", scatter_dimension=0, tiled=True).reshape(n_seq, rows, -1)
    gqkv = lax.all_to_all(gqkv, "seq", split_axis=0, concat_axis=0, tiled=True)
    dn1 = lax.psum_scatter(dn1p, "seq", scatter_dimension=0, tiled=True).astype(F32)
    r1 = rms_factor(xo)
    dg1 = dn1 * gain_one
    gin = dmixed + r1 * dg1 - xo * r1**3 * jnp.mean(dg1 * xo, axis=-1, keepdims=True)

    gqkv = gqkv.astype(F32)
    g_query = gqkv[:, :, :nq].transpose(1, 0, 2).reshape(rows, -1)
    g_key = gqkv[:, :, nq: nq + nk].transpose(1, 0, 2).reshape(rows, -1)
    g_value = gqkv[:, :, nq + nk: nqkv].transpose(1, 0, 2).reshape(rows, -1)
    g_router = jnp.sum(gqkv[:, :, nqkv: nqkv + experts] + gqkv[:, :, nqkv + experts: nqkv + 2 * experts], axis=0)
    ggu = ggu.astype(F32).reshape(n_seq, rows, 2, experts, fc).transpose(2, 3, 1, 0, 4).reshape(2, experts, rows, ff)
    g_gate, g_up = ggu[0], ggu[1]
    g_gain_one = (
        jnp.sum(w_query.astype(F32) * g_query, axis=1) + jnp.sum(w_key.astype(F32) * g_key, axis=1)
        + jnp.sum(w_value.astype(F32) * g_value, axis=1)
    ) / gain_attn.astype(F32)
    g_gain_two = (
        jnp.sum(w_gate.astype(F32) * g_gate + w_up.astype(F32) * g_up, axis=(0, 2))
        + jnp.sum(router.astype(F32) * g_router, axis=1)
    ) / gain_ffn.astype(F32)
    return (
        output[None], gin.astype(BF)[None], g_gain_one, g_query, g_key, g_value, gwo.astype(F32), g_gain_two, g_router,
        g_gate, g_up, gwd.astype(F32).reshape(experts, ff_rows, d),
    )


def solution(mesh):
    tok = P("fsdp", "seq", None)
    vec = P(("seq", "fsdp"))
    mat = P(("seq", "fsdp"), None)
    exp = P(None, ("seq", "fsdp"), None)
    return jax.shard_map(
        shards,
        mesh=mesh,
        in_specs=(tok, tok, tok, vec, mat, mat, mat, mat, vec, mat, exp, exp, exp),
        out_specs=(tok, tok, vec, mat, mat, mat, mat, vec, mat, exp, exp, exp),
        check_vma=False,
    )
```

time: 2640 us -> 809 us (0.31)
  waiting for transfers between devices: 2090 us -> 454 us
  blocking collectives: 150 us -> 40.8 us
  matrix products: 212 us -> 158 us
  local copies, waits for them, and re-layouts: 89.9 us -> 60 us
    reduce_scatter x16 -> x8, waiting for transfers between devices: 1740 us -> 232 us  [the longest x1 46.2 us: shards(): lax.psum_scatter(dn2p, 'seq', scatter_dimension=0, tiled=True).astype(F32)]
    all_gather x7, waiting for transfers between devices: 328 us -> 207 us  [the longest x1 58.7 us: shards(): gu = lax.all_gather(gu, 'fsdp', axis=1).reshape(d, -1)]
    unnamed x2 -> x0, blocking collectives: 79.9 us -> none
    dot_general x46 -> x21, matrix products: 211 us -> 158 us  [the longest x5 39.5 us: dot_t(): lax.dot_general(a, b, (((1,), (1,)), ((), ())), preferred_element_type=F32)]
    all_gather x1, blocking collectives: 40.9 us -> 8.01 us  [shards(): ids = lax.all_gather(routes[0], 'seq', axis=0, tiled=True)]
  transfers between devices with their start and end apart: 29 -> 18, of which waited for: 23 -> 15; matrix products, arithmetic and copies ran while one was open for 11% -> 29% of each run, Pallas kernels for 0% -> 0%
where the time goes in v1:
time: 809 us; the launch traced here: 799 us
  waiting for transfers between devices  454 us (56%)
  matrix products  158 us (20%)
  other arithmetic  62.2 us (8%)
  local copies, waits for them, and re-layouts  60 us (7%)
  blocking collectives  40.8 us (5%)
  between operations  14.8 us (2%)
  starting transfers between devices  9.8 us (1%)
    all_gather x1, waiting for transfers between devices, shards(): gu = lax.all_gather(gu, 'fsdp', axis=1).reshape(d, -1)  58.7 us
    reduce_scatter x1, waiting for transfers between devices, shards(): lax.psum_scatter(dn2p, 'seq', scatter_dimension=0, tiled=True).astype(F32)  46.2 us
    reduce_scatter x1, waiting for transfers between devices, shards(): out = lax.psum_scatter(outp, 'seq', scatter_dimension=0, tiled=True)  45.5 us
    reduce_scatter x1, waiting for transfers between devices, shards(): mine = lax.psum_scatter(part, 'seq', scatter_dimension=0, tiled=True)  42.8 us
    all_gather x1, waiting for transfers between devices, shards(): xs = lax.all_gather(x[0], 'seq', axis=0, tiled=True)  41.2 us
    dot_general x5, matrix products, dot_t(): lax.dot_general(a, b, (((1,), (1,)), ((), ())), preferred_element_type=F32)  39.5 us
    reduce_scatter x1, waiting for transfers between devices, shards(): lax.psum_scatter(dn1p, 'seq', scatter_dimension=0, tiled=True).astype(F32)  34.4 us
    reduce_scatter x1, waiting for transfers between devices, shards(): lax.psum_scatter(gqkv, 'fsdp', scatter_dimension=0, tiled=True)  33.1 us
  transfers between devices with their start and end apart: 18, of which 15 were waited for; matrix products, arithmetic and copies ran while one was open for 29% of the time, Pallas kernels for 0%

profile of v1, /device:TPU:0, one launch (start us, length us, event | category | flops | bytes accessed | tf_op | source)
XLA Modules:
  0.0 799.4 jit_solution(8273309121592372966)
XLA Ops:
  12.6 11.3 %all_to_all.20 = bf16[4,48,768]{2,1,0:T(8,128)(2,1)S(1)} all-to-all(bf16[4,48,768]{2,1,0:T(8,128)(2,1)S(1)} %copy.105), channel_id=1, replica_groups=mesh['seq'=4,'fsdp'=8] {'seq'}, dimensions={0} | all-to-all | bytes 589824 | tf_op jit(solution)/shard_map/all_to_all | solution.py:57
  26.8 29.2 %all-gather.20.cloned.1.call-done = bf16[4,384,768]{2,0,1:T(4,128)(2,1)} async-done(((bf16[4,48,768]{2,0,1:T(4,128)(2,1)}), bf16[4,384,768]{2,0,1:T(4,128)(2,1)}) %all-gather.20.cloned.1.call-update) | async-done | bytes 2359312 | tf_op jit(solution)/shard_map/all_gather | solution.py:60
  56.0 2.0 copy.107
  59.8 41.2 %all-gather.18.cloned.1.call-done = bf16[1,1024,1536]{2,1,0:T(8,128)(2,1)} async-done(((bf16[1,256,1536]{2,1,0:T(8,128)(2,1)}), bf16[1,1024,1536]{2,1,0:T(8,128)(2,1)}) %all-gather.18.cloned.1.call-update) | async-done | bytes 3145744 | tf_op jit(solution)/shard_map/all_gather | solution.py:73
  101.0 2.7 fusion.9
  103.7 4.4 fusion.21
  108.2 10.7 %fusion.59 = (f32[2,3,1024]{2,1,0:T(4,128)S(1)}, f32[2,3,1024,1024]{2,3,1,0:T(8,128)}) fusion(bf16[1024,2,64,1]{0,2,3,1:T(8,128)(2,1)S(1)} %bitcast.195, bf16[1024,2,3,64]{0,3,2,1:T(8,128)(2,1)S(1)} %bitcast.172, pred[1024,1024]{0,1:T(8,128)(4,1)S(1)} %iota_compare_fusion), kind=kOutput, calls=%fused_computation.122 | convolution fusion | flops 824174592 | bytes 27287552 | tf_op jit(solution)/shard_map/qgrd,kgd->grqk/dot_general | solution.py:33
  118.9 10.3 %fusion.3 = f32[2,3,1024]{2,1,0:T(4,128)S(1)} fusion(f32[2,3,1024,1024]{2,3,1,0:T(8,128)} %get-tuple-element.65, f32[2,3,1024]{2,1,0:T(4,128)S(1)} %get-tuple-element.64), kind=kLoop, calls=%fused_computation.9 | loop fusion | flops 12576768 | bytes 25214976 | tf_op jit(solution)/shard_map/reduce_sum | solution.py:86
  129.2 10.8 %fusion.30 = bf16[2,64,3,1024]{3,1,2,0:T(8,128)(2,1)S(1)} fusion(bf16[1024,2,64,1]{0,2,3,1:T(8,128)(2,1)S(1)} %bitcast.201, f32[2,3,1024,1024]{2,3,1,0:T(8,128)} %get-tuple-element.65, f32[2,3,1024]{2,1,0:T(4,128)S(1)} %fusion.3, f32[2,3,1024]{2,1,0:T(4,128)S(1)} %get-tuple-element.64), kind=kOutput, calls=%fused_computation.65 | convolution fusion | flops 824573952 | bytes 26263552 | tf_op jit(solution)/shard_map/grqk,kgd->qgrd/dot_general | solution.py:89
  140.0 11.7 %all-gather.22.cloned.1.call-done = bf16[1408,1536]{1,0:T(8,128)(2,1)} async-done(((bf16[176,1536]{1,0:T(8,128)(2,1)}), bf16[1408,1536]{1,0:T(8,128)(2,1)}) %all-gather.22.cloned.1.call-update) | async-done | bytes 4325392 | tf_op jit(solution)/shard_map/all_gather | solution.py:61
  154.1 3.5 convolution_convert_fusion.3
  157.6 42.8 %reduce-scatter.12.cloned.1.call-done = bf16[256,1536]{1,0:T(8,128)(2,1)} async-done(((bf16[1024,1536]{1,0:T(8,128)(2,1)}), bf16[256,1536]{1,0:T(8,128)(2,1)}) %reduce-scatter.12.cloned.1.call-update) | async-done | bytes 786448 | tf_op jit(solution)/shard_map/reduce_scatter | solution.py:91
  201.9 2.3 multiply_convert_fusion.4
  206.8 21.5 %all_to_all.21 = bf16[4,48,2048]{2,1,0:T(8,128)(2,1)} all-to-all(bf16[4,48,2048]{2,1,0:T(8,128)(2,1)S(1)} %reshape.222), channel_id=1, replica_groups=mesh['seq'=4,'fsdp'=8] {'seq'}, dimensions={0} | all-to-all | bytes 1572864 | tf_op jit(solution)/shard_map/all_to_all | solution.py:58
  229.1 8.0 %all-gather.3 = s32[1,1024,2]{1,2,0:T(2,128)S(1)} all-gather(s32[1,256,2]{1,2,0:T(2,128)S(1)} %copy-done.24), channel_id=5, replica_groups=mesh['seq'=4,'fsdp'=8] {'seq'}, dimensions={1}, use_global_device_ids=true | all-gather | bytes 10240 | tf_op jit(solution)/shard_map/all_gather | solution.py:75
  237.1 2.1 slice.84
  239.2 2.0 copy.112
  241.2 13.0 %all-gather.14.cloned.1.call-done = bf16[1024,1536]{1,0:T(8,128)(2,1)} async-done(((bf16[256,1536]{1,0:T(8,128)(2,1)}), bf16[1024,1536]{1,0:T(8,128)(2,1)}) %all-gather.14.cloned.1.call-update) | async-done | bytes 3145744 | tf_op jit(solution)/shard_map/all_gather | solution.py:97
  254.1 2.9 select_reduce_fusion
  258.6 3.0 copy.143
  261.6 58.7 %all-gather.24.cloned.1.call-done = bf16[4,384,2048]{2,1,0:T(8,128)(2,1)} async-done(((bf16[4,48,2048]{2,1,0:T(8,128)(2,1)}), bf16[4,384,2048]{2,1,0:T(8,128)(2,1)}) %all-gather.24.cloned.1.call-update) | async-done | bytes 6291472 | tf_op jit(solution)/shard_map/all_gather | solution.py:64
  320.3 11.6 %fusion.60 = f32[1024,2048]{1,0:T(8,128)} fusion(bf16[1024,1536]{1,0:T(8,128)(2,1)} %all-gather.14.cloned.1.call-done, bf16[1536,2048]{1,0:T(8,128)(2,1)} %bitcast.216), kind=kOutput, calls=%fused_computation.123 | convolution fusion | flops 6442450944 | bytes 17825792 | tf_op jit(solution)/shard_map/dot_general | solution.py:16
  332.0 32.9 %all-gather.26.cloned.1.call-done = bf16[1,1024,1536]{2,1,0:T(8,128)(2,1)} async-done(((bf16[1,256,1536]{2,1,0:T(8,128)(2,1)}), bf16[1,1024,1536]{2,1,0:T(8,128)(2,1)}) %all-gather.26.cloned.1.call-update) | async-done | bytes 3145744 | tf_op jit(solution)/shard_map/all_gather | solution.py:74
  364.9 15.4 %multiply_convert_fusion.1 = (bf16[1024,1024]{1,0:T(8,128)(2,1)}, bf16[1024,1024]{1,0:T(8,128)(2,1)}, f32[1024,1024]{1,0:T(8,128)}, bf16[1024,1024]{1,0:T(8,128)(2,1)}) fusion(f32[1024,2048]{1,0:T(8,128)} %fusion.60, f32[1024,1024]{1,0:T(8,128)} %bitcast.187, bf16[1024,1536]{1,0:T(8,128)(2,1)} %bitcast.192, ...), kind=kOutput, calls=%fused_computation.26 | convolution fusion | flops 3240099840 | bytes 29360128 | tf_op jit(solution)/shard_map/dot_general | solution.py:20
  380.2 5.6 reshape.226
  385.9 4.2 reduce_sum.148
  390.5 11.3 %convolution_convert_fusion.1 = bf16[1024,1536]{1,0:T(8,128)(2,1)} fusion(bf16[1536,2048]{1,0:T(8,128)(2,1)} %bitcast.217, bf16[1024,1024]{1,0:T(8,128)(2,1)} %get-tuple-element.49, bf16[1024,1024]{1,0:T(8,128)(2,1)} %get-tuple-element.48), kind=kOutput, calls=%fused_computation.31 | convolution fusion | flops 6452412416 | bytes 13631488 | tf_op jit(solution)/shard_map/dot_general | solution.py:20
  401.9 13.1 %reduce-scatter.28.cloned.1.call-done = f32[256,4]{1,0:T(8,128)} async-done(((f32[1024,4]{1,0:T(8,128)}), f32[256,4]{1,0:T(8,128)}) %reduce-scatter.28.cloned.1.call-update) | async-done | bytes 4112
  416.0 46.2 %reduce-scatter.16.cloned.1.call-done = bf16[256,1536]{1,0:T(8,128)(2,1)} async-done(((bf16[1024,1536]{1,0:T(8,128)(2,1)}), bf16[256,1536]{1,0:T(8,128)(2,1)}) %reduce-scatter.16.cloned.1.call-update) | async-done | bytes 786448 | tf_op jit(solution)/shard_map/reduce_scatter | solution.py:129
  462.2 2.0 multiply_reduce_fusion
  464.3 2.5 fusion.56
  466.9 9.7 %convolution_convert_fusion = bf16[1536,2048]{1,0:T(8,128)(2,1)S(1)} fusion(bf16[1024,1536]{1,0:T(8,128)(2,1)} %all-gather.14.cloned.1.call-done, bf16[1024,1024]{1,0:T(8,128)(2,1)} %get-tuple-element.49, bf16[1024,1024]{1,0:T(8,128)(2,1)} %get-tuple-element.48), kind=kOutput, calls=%fused_computation.16 | convolution fusion | flops 6453985280 | bytes 13631488 | tf_op jit(solution)/shard_map/dot_general | solution.py:24
  476.6 3.2 copy.123
  480.0 7.2 convolution_convert_fusion.4
  487.2 1.9 copy.127
  490.5 20.5 %all-gather.16.cloned.1.call-done = bf16[1024,1536]{1,0:T(8,128)(2,1)} async-done(((bf16[256,1536]{1,0:T(8,128)(2,1)}), bf16[1024,1536]{1,0:T(8,128)(2,1)}) %all-gather.16.cloned.1.call-update) | async-done | bytes 3145744 | tf_op jit(solution)/shard_map/all_gather | solution.py:140
  511.0 4.5 convolution_convert_fusion.8
  515.5 16.4 %fusion = (f32[2,3,1024]{2,1,0:T(4,128)S(1)}, f32[2,1024,1024,3]{2,1,3,0:T(8,128)}) fusion(f32[2,3,1024,1024]{2,3,1,0:T(8,128)} %get-tuple-element.65, f32[2,3,1024]{2,1,0:T(4,128)S(1)} %log_add_fusion, bf16[1024,2,64,1]{0,2,3,1:T(8,128)(2,1)S(1)} %bitcast.202, bf16[1024,2,3,64]{0,3,2,1:T(8,128)(2,1)} %bitcast.190), kind=kOutput, calls=%fused_computation.2 | convolution fusion | flops 824174592 | bytes 51429376 | tf_op jit(solution)/shard_map/qgrd,kgd->grqk/dot_general | solution.py:145
  531.9 17.5 %fusion.2 = bf16[2,3,1024,1024]{2,3,1,0:T(8,128)(2,1)S(1)} fusion(f32[2,1024,1024,3]{2,1,3,0:T(8,128)} %get-tuple-element.71, f32[2,3,1024,1024]{2,3,1,0:T(8,128)} %get-tuple-element.65, f32[2,3,1024]{2,1,0:T(4,128)S(1)} %get-tuple-element.70, f32[2,3,1024]{2,1,0:T(4,128)S(1)} %log_add_fusion), kind=kLoop, calls=%fused_computation.4 | loop fusion | flops 25165824 | bytes 62963712 | tf_op jit(solution)/shard_map/convert_element_type | solution.py:147
  549.4 3.2 multiply_convert_fusion.3
  552.6 5.1 fusion.35
  557.7 13.3 %fusion.36 = bf16[2,64,1024]{2,1,0:T(8,128)(2,1)} fusion(bf16[1024,2,3,64]{0,3,2,1:T(8,128)(2,1)} %bitcast.191, f32[2,3,1024,1024]{2,3,1,0:T(8,128)} %get-tuple-element.65, f32[2,3,1024]{2,1,0:T(4,128)S(1)} %log_add_fusion), kind=kOutput, calls=%fused_computation.72 | convolution fusion | flops 818020352 | bytes 26238976 | tf_op jit(solution)/shard_map/grqk,qgrd->kgd/dot_general | solution.py:150
  571.0 4.6 convolution_convert_fusion.6
  575.6 1.8 maximum_maximum_fusion
  577.4 4.3 copy.118
  581.7 3.3 copy.119
  585.1 4.6 convolution_convert_fusion.7
  589.9 6.3 convolution_convert_fusion.2
  596.3 8.9 %convolution_convert_fusion.5 = bf16[1024,1536]{1,0:T(8,128)(2,1)} fusion(bf16[1024,1536]{1,0:T(8,128)(2,1)} %bitcast.193, f32[1024,1024]{1,0:T(8,128)} %bitcast.189, bf16[1024,1024]{1,0:T(8,128)(2,1)} %get-tuple-element.51), kind=kOutput, calls=%fused_computation.35 | convolution fusion | flops 3225944064 | bytes 12582912 | tf_op jit(solution)/shard_map/dot_general | solution.py:16
  605.3 4.3 all-to-all-start.3
  610.2 14.0 %reduce-scatter.26.cloned.1.call-done = bf16[128,1536]{1,0:T(8,128)(2,1)} async-done(((bf16[1024,1536]{1,0:T(8,128)(2,1)}), bf16[128,1536]{1,0:T(8,128)(2,1)}) %reduce-scatter.26.cloned.1.call-update) | async-done | bytes 393232 | tf_op jit(solution)/shard_map/reduce_scatter | solution.py:122
  624.3 2.0 convert.8
  626.2 3.1 reshape.249
  629.3 33.1 %reduce-scatter.20.cloned.1.call-done = bf16[192,768]{1,0:T(8,128)(2,1)} async-done(((bf16[1536,768]{1,0:T(8,128)(2,1)}), bf16[192,768]{1,0:T(8,128)(2,1)}) %reduce-scatter.20.cloned.1.call-update) | async-done | bytes 294928 | tf_op jit(solution)/shard_map/reduce_scatter | solution.py:160
  662.3 4.1 all-to-all-start.2
  666.4 2.5 fusion.57
  670.4 2.4 squeeze.22
  672.8 2.5 copy.125
  675.3 2.4 squeeze.23
  677.7 2.3 add_reduce_fusion
  680.0 16.4 %reduce-scatter.22.cloned.1.call-done = bf16[48,1536]{1,0:T(8,128)(2,1)} async-done(((bf16[384,1536]{1,0:T(8,128)(2,1)}), bf16[48,1536]{1,0:T(8,128)(2,1)}) %reduce-scatter.22.cloned.1.call-update) | async-done | bytes 147472 | tf_op jit(solution)/shard_map/reduce_scatter | solution.py:142
  707.2 34.4 %reduce-scatter.18.cloned.1.call-done = bf16[256,1536]{1,0:T(8,128)(2,1)} async-done(((bf16[1024,1536]{1,0:T(8,128)(2,1)}), bf16[256,1536]{1,0:T(8,128)(2,1)}) %reduce-scatter.18.cloned.1.call-update) | async-done | bytes 786448 | tf_op jit(solution)/shard_map/reduce_scatter | solution.py:162
  743.2 45.5 %reduce-scatter.14.cloned.1.call-done = bf16[256,1536]{1,0:T(8,128)(2,1)} async-done(((bf16[1024,1536]{1,0:T(8,128)(2,1)}), bf16[256,1536]{1,0:T(8,128)(2,1)}) %reduce-scatter.14.cloned.1.call-update) | async-done | bytes 786448 | tf_op jit(solution)/shard_map/reduce_scatter | solution.py:127
  788.8 3.8 fusion.42
  (148 shorter events, 37.0 us)
Async XLA Ops:
  7.2 18.4 %copy-start.13 = (bf16[4,32,1536]{2,1,0:T(8,128)(2,1)S(1)}, bf16[4,32,1536]{2,1,0:T(8,128)(2,1)}, u32[]{:S(2)}) copy-start(bf16[4,32,1536]{2,1,0:T(8,128)(2,1)} %param.25) | copy-start | bytes 1179652
  7.2 18.4 %copy-start.15 = (bf16[48,1536]{1,0:T(8,128)(2,1)S(1)}, bf16[48,1536]{1,0:T(8,128)(2,1)}, u32[]{:S(2)}) copy-start(bf16[48,1536]{1,0:T(8,128)(2,1)} %param.20) | copy-start | bytes 442372
  7.2 48.8 %all-gather.20.cloned.1.call-start = ((), (), s32[]{:S(2)}) async-start(), calls=%async_computation.24 | async-start | bytes 2654208 | tf_op jit(solution)/shard_map/all_gather | solution.py:60
  24.8 76.2 %all-gather.18.cloned.1.call-start = ((), (), s32[]{:S(2)}) async-start(), calls=%async_computation.23 | async-start | bytes 3932160 | tf_op jit(solution)/shard_map/all_gather | solution.py:73
  25.5 126.2 %all-gather.22.cloned.1.call-start = ((), (), s32[]{:S(2)}) async-start(), calls=%async_computation.25 | async-start | bytes 4866048 | tf_op jit(solution)/shard_map/all_gather | solution.py:61
  26.4 174.0 %reduce-scatter.12.cloned.1.call-start = ((), (), s32[]{:S(2)}) async-start(), calls=%async_computation.13 | async-start | bytes 3932160 | tf_op jit(solution)/shard_map/reduce_scatter | solution.py:91
  58.0 1.4 copy-start.3
  59.8 48.3 %copy-start.16 = (f32[1536]{0:T(1024)}, f32[1536]{0:T(1024)S(1)}, u32[]{:S(2)}) copy-start(f32[1536]{0:T(1024)S(1)} %get-tuple-element.37) | copy-start | bytes 18436
  101.0 2.7 copy-start.4
  103.7 4.4 copy-start.20
  108.1 10.7 %copy-start.2 = (bf16[1024,384]{0,1:T(8,128)(2,1)}, bf16[1024,384]{0,1:T(8,128)(2,1)S(1)}, u32[]{:S(2)}) copy-start(bf16[1024,384]{0,1:T(8,128)(2,1)S(1)} %slice.78) | copy-start | bytes 2359300
  108.2 10.7 %copy-start.6 = (bf16[1024,128]{0,1:T(8,128)(2,1)}, bf16[1024,128]{0,1:T(8,128)(2,1)S(1)}, u32[]{:S(2)}) copy-start(bf16[1024,128]{0,1:T(8,128)(2,1)S(1)} %get-tuple-element.56) | copy-start | bytes 786436
  140.0 17.6 %copy-start.27 = (bf16[2,64,3,1024]{3,1,2,0:T(8,128)(2,1)}, bf16[2,64,3,1024]{3,1,2,0:T(8,128)(2,1)S(1)}, u32[]{:S(2)}) copy-start(bf16[2,64,3,1024]{3,1,2,0:T(8,128)(2,1)S(1)} %fusion.30) | copy-start | bytes 2359300
  153.0 1.0 copy-start.11
  157.5 42.9 %copy-start = (bf16[1,256,1536]{2,1,0:T(8,128)(2,1)S(1)}, bf16[1,256,1536]{2,1,0:T(8,128)(2,1)}, u32[]{:S(2)}) copy-start(bf16[1,256,1536]{2,1,0:T(8,128)(2,1)} %param.13) | copy-start | bytes 2359300
  157.6 46.9 %copy-start.10 = (bf16[4,48,1024]{2,1,0:T(8,128)(2,1)S(1)}, bf16[4,48,1024]{2,1,0:T(8,128)(2,1)}, u32[]{:S(2)}) copy-start(bf16[4,48,1024]{2,1,0:T(8,128)(2,1)} %param.23) | copy-start | bytes 1179652
  157.6 47.5 %copy-start.8 = (bf16[4,48,1024]{2,1,0:T(8,128)(2,1)S(1)}, bf16[4,48,1024]{2,1,0:T(8,128)(2,1)}, u32[]{:S(2)}) copy-start(bf16[4,48,1024]{2,1,0:T(8,128)(2,1)} %param.24) | copy-start | bytes 1179652
  157.6 96.6 %all-gather.14.cloned.1.call-start = ((), (), s32[]{:S(2)}) async-start(), calls=%async_computation.14 | async-start | bytes 3932160 | tf_op jit(solution)/shard_map/all_gather | solution.py:97
  204.2 116.1 %all-gather.24.cloned.1.call-start = ((), (), s32[]{:S(2)}) async-start(), calls=%async_computation.26 | async-start | bytes 7077888 | tf_op jit(solution)/shard_map/all_gather | solution.py:64
  205.7 23.4 %copy-start.24 = (s32[1,256,2]{1,2,0:T(2,128)S(1)}, s32[1,256,2]{1,2,0:T(2,128)}, u32[]{:S(2)}) copy-start(s32[1,256,2]{1,2,0:T(2,128)} %param.15) | copy-start | bytes 6148
  228.3 136.6 %all-gather.26.cloned.1.call-start = ((), (), s32[]{:S(2)}) async-start(), calls=%async_computation.27 | async-start | bytes 3932160 | tf_op jit(solution)/shard_map/all_gather | solution.py:74
  229.0 186.0 %reduce-scatter.28.cloned.1.call-start = ((), (), s32[]{:S(2)}) async-start(), calls=%async_computation.28 | async-start | bytes 655360
  390.1 72.2 %reduce-scatter.16.cloned.1.call-start = ((), (), s32[]{:S(2)}) async-start(), calls=%async_computation.16 | async-start | bytes 3932160 | tf_op jit(solution)/shard_map/reduce_scatter | solution.py:129
  401.8 60.4 %copy-start.1 = (bf16[256,1536]{1,0:T(8,128)(2,1)S(1)}, bf16[256,1536]{1,0:T(8,128)(2,1)}, u32[]{:S(2)}) copy-start(bf16[256,1536]{1,0:T(8,128)(2,1)} %reduce-scatter.12.cloned.1.call-done) | copy-start | bytes 2359300
  401.9 109.1 %all-gather.16.cloned.1.call-start = ((), (), s32[]{:S(2)}) async-start(), calls=%async_computation.17 | async-start | bytes 3932160 | tf_op jit(solution)/shard_map/all_gather | solution.py:140
  464.3 12.3 %copy-start.18 = (f32[256]{0:T(256)}, f32[256]{0:T(256)S(1)}, u32[]{:S(2)}) copy-start(f32[256]{0:T(256)S(1)} %broadcast_multiply_fusion.1) | copy-start | bytes 3076
  466.9 138.4 %reduce-scatter.24.cloned.1.call-start = ((), (), s32[]{:S(2)}) async-start(), calls=%async_computation.21 | async-start | bytes 7077888 | tf_op jit(solution)/shard_map/reduce_scatter | solution.py:124
  479.8 144.4 %reduce-scatter.26.cloned.1.call-start = ((), (), s32[]{:S(2)}) async-start(), calls=%async_computation.22 | async-start | bytes 3538944 | tf_op jit(solution)/shard_map/reduce_scatter | solution.py:122
  489.1 173.2 %reduce-scatter.20.cloned.1.call-start = ((), (), s32[]{:S(2)}) async-start(), calls=%async_computation.19 | async-start | bytes 2654208 | tf_op jit(solution)/shard_map/reduce_scatter | solution.py:160
  531.9 17.5 %copy-start.7 = (bf16[1024,128]{0,1:T(8,128)(2,1)S(1)}, bf16[1024,128]{0,1:T(8,128)(2,1)}, u32[]{:S(2)}) copy-start(bf16[1024,128]{0,1:T(8,128)(2,1)} %copy-done.6) | copy-start | bytes 786436
  557.7 13.3 %copy-start.17 = (f32[1536]{0:T(1024)S(1)}, f32[1536]{0:T(1024)}, u32[]{:S(2)}) copy-start(f32[1536]{0:T(1024)} %copy-done.16) | copy-start | bytes 18436
  557.7 13.3 %copy-start.21 = (f32[1024]{0:T(1024)S(1)}, f32[1024]{0:T(1024)}, u32[]{:S(2)}) copy-start(f32[1024]{0:T(1024)} %copy-done.20) | copy-start | bytes 12292
  585.1 111.3 %reduce-scatter.22.cloned.1.call-start = ((), (), s32[]{:S(2)}) async-start(), calls=%async_computation.20 | async-start | bytes 1327104 | tf_op jit(solution)/shard_map/reduce_scatter | solution.py:142
  589.7 152.0 %reduce-scatter.18.cloned.1.call-start = ((), (), s32[]{:S(2)}) async-start(), calls=%async_computation.18 | async-start | bytes 3932160 | tf_op jit(solution)/shard_map/reduce_scatter | solution.py:162
  596.2 192.5 %reduce-scatter.14.cloned.1.call-start = ((), (), s32[]{:S(2)}) async-start(), calls=%async_computation.15 | async-start | bytes 3932160 | tf_op jit(solution)/shard_map/reduce_scatter | solution.py:127
  605.2 4.3 copy-start.22
  605.3 20.9 %all-to-all-start.3 = ((bf16[4,48,2048]{2,1,0:T(8,128)(2,1)}), bf16[4,48,2048]{2,1,0:T(8,128)(2,1)}, u32[]{:S(2)}, u32[]{:S(2)}) async-start(bf16[4,48,2048]{2,1,0:T(8,128)(2,1)} %bitcast.205), calls=%async_computation.10 | async-start | bytes 1572864 | tf_op jit(solution)/shard_map/all_to_all | solution.py:125
  662.3 35.7 %all-to-all-start.2 = ((bf16[4,48,768]{2,1,0:T(8,128)(2,1)}), bf16[4,48,768]{2,1,0:T(8,128)(2,1)}, u32[]{:S(2)}, u32[]{:S(2)}) async-start(bf16[4,48,768]{2,1,0:T(8,128)(2,1)} %bitcast.210), calls=%async_computation.7 | async-start | bytes 589824 | tf_op jit(solution)/shard_map/all_to_all | solution.py:161
  669.0 8.7 %copy-start.9 = (bf16[4,48,1024]{2,1,0:T(8,128)(2,1)S(1)}, bf16[4,48,1024]{2,1,0:T(8,128)(2,1)}, u32[]{:S(2)}) copy-start(bf16[4,48,1024]{2,1,0:T(8,128)(2,1)} %param.24) | copy-start | bytes 1179652
  680.0 23.6 %copy-start.23 = (f32[48]{0:T(128)S(1)}, f32[48]{0:T(128)}, u32[]{:S(2)}) copy-start(f32[48]{0:T(128)} %add_reduce_fusion) | copy-start | bytes 580
  680.0 23.6 %copy-start.26 = (bf16[48]{0:T(256)(128)(2,1)S(1)}, bf16[48]{0:T(256)(128)(2,1)}, u32[]{:S(2)}) copy-start(bf16[48]{0:T(256)(128)(2,1)} %param.21) | copy-start | bytes 292
  680.0 25.1 %copy-start.14 = (bf16[48,512]{1,0:T(8,128)(2,1)S(1)}, bf16[48,512]{1,0:T(8,128)(2,1)}, u32[]{:S(2)}) copy-start(bf16[48,512]{1,0:T(8,128)(2,1)} %param.19) | copy-start | bytes 147460
  680.0 26.7 %copy-start.25 = (bf16[48]{0:T(256)(128)(2,1)S(1)}, bf16[48]{0:T(256)(128)(2,1)}, u32[]{:S(2)}) copy-start(bf16[48]{0:T(256)(128)(2,1)} %param.16) | copy-start | bytes 292
  680.0 108.7 %copy-start.19 = (f32[256]{0:T(256)S(1)}, f32[256]{0:T(256)}, u32[]{:S(2)}) copy-start(f32[256]{0:T(256)} %copy-done.18) | copy-start | bytes 3076
  699.1 0.8 copy-start.5
  701.6 91.0 %copy-start.12 = (f32[4,6,8,384]{3,2,0,1:T(8,128)}, f32[4,6,8,384]{3,2,0,1:T(8,128)S(1)}, u32[]{:S(2)}) copy-start(f32[4,6,8,384]{3,2,0,1:T(8,128)S(1)} %copy.140) | copy-start | bytes 884740
Sparse Core Ops, SparseCore 0:
  24.9 31.0 all-gather.19
  57.8 43.0 all-gather.17
  103.2 48.4 all-gather.21
  157.7 42.6 reduce-scatter.11
  204.3 49.7 all-gather.13
  255.6 64.6 all-gather.23
  322.2 42.6 all-gather.25
  390.2 24.7 reduce-scatter.27
  418.3 43.9 reduce-scatter.15
  467.0 43.9 all-gather.15
  513.4 69.8 reduce-scatter.23
  585.5 38.6 reduce-scatter.25
  626.7 35.6 reduce-scatter.19
  664.6 31.7 reduce-scatter.21
  699.5 42.1 reduce-scatter.17
  744.8 43.9 reduce-scatter.13

commit v2 on v1

v2 whole, which is shorter than its diff:
```python
import functools

import jax
import jax.numpy as jnp
from jax import lax
from jax.experimental import pallas as pl
from jax.experimental.pallas import tpu as pltpu
from jax.sharding import PartitionSpec as P

HEAD_DIM = 64
EPS = 1e-06
SCALE = HEAD_DIM ** (-0.5)
BF = jnp.bfloat16
F32 = jnp.float32
MESH = pl.DeviceIdType.MESH
ANY = pl.BlockSpec(memory_space=pl.ANY)
VM = pl.BlockSpec(memory_space=pltpu.VMEM)
MIB = 2**20


def dot(a, b):
    return jnp.dot(a, b, preferred_element_type=F32)


def dot_t(a, b):
    return lax.dot_general(a, b, (((1,), (1,)), ((), ())), preferred_element_type=F32)


def t_dot(a, b):
    return lax.dot_general(a, b, (((0,), (0,)), ((), ())), preferred_element_type=F32)


def rms_factor(rows):
    return lax.rsqrt(jnp.mean(rows * rows, axis=-1, keepdims=True) + EPS)


def partner(me, step):
    return ((me // 2 + step // 2) % 2) * 2 + (me % 2 + step % 2) % 2


def send(src, dst, sems, slot, peer):
    return pltpu.make_async_remote_copy(
        src_ref=src, dst_ref=dst, send_sem=sems.at[0, slot], recv_sem=sems.at[1, slot],
        device_id={"seq": peer}, device_id_type=MESH,
    )


def greet(me):
    barrier = pltpu.get_barrier_semaphore()
    for step in (1, 2, 3):
        pl.semaphore_signal(barrier, inc=1, device_id={"seq": partner(me, step)}, device_id_type=MESH)
    pl.semaphore_wait(barrier, 3)


class Gather:
    def __init__(self, me, own, buf, sems, base=0):
        rows = own.shape[0]
        half = rows // 2
        one, two = partner(me, 1), partner(me, 2)

        def part(owner, start, size):
            return buf.at[pl.ds(pl.multiple_of(owner * rows + start, half), size)]

        mine = part(me, 0, rows)
        self.first = send(own, mine, sems, base, one)
        self.second = send(own, mine, sems, base + 1, two)
        onward = part(one, 0, half)
        self.third = send(onward, onward, sems, base + 2, two)
        onward = part(two, half, half)
        self.fourth = send(onward, onward, sems, base + 3, one)

    def start(self):
        self.first.start()
        self.second.start()

    def got_one(self):
        self.first.wait_recv()
        self.third.start()

    def got_two(self):
        self.second.wait_recv()
        self.fourth.start()

    def got_three(self):
        self.third.wait_recv()
        self.fourth.wait_recv()

    def finish(self):
        for copy in (self.first, self.second, self.third, self.fourth):
            copy.wait_send()


def lanes(shape):
    return lax.broadcasted_iota(jnp.int32, shape, len(shape) - 1)


def pack_two(value, experts):
    high = value.astype(BF).astype(F32)
    low = value - high
    return jnp.where(lanes(value.shape) < experts, high, pltpu.roll(low, experts, 1)).astype(BF)


def front_kernel(
    nq, nk, experts, x_ref, g_ref, gain_ref, named_ref, wqkv_ref, wo_ref, wr_ref,
    n1_ref, qkv_ref, attn_ref, lse_ref, mixed_ref, n2_ref, gate_ref, gs_ref,
    xs_ref, send_ref, recv_ref, xsem, gsem, asem, lsem,
):
    me = lax.axis_index("seq")
    toks = x_ref.shape[0]
    group = nq // nk
    greet(me)
    xg = Gather(me, x_ref, xs_ref, xsem)
    xg.start()
    keep = pltpu.make_async_copy(g_ref, gs_ref.at[pl.ds(pl.multiple_of(me * toks, toks), toks)], lsem)
    keep.start()
    gg = Gather(me, g_ref, gs_ref, gsem)
    gain1 = gain_ref[0:1, :]

    @pl.loop(0, 4)
    def _(step):
        block = partner(me, step)
        rows = pl.ds(pl.multiple_of(block * toks, toks), toks)

        @pl.when(step == 0)
        def _():
            xs_ref[rows, :] = x_ref[...]

        @pl.when(step == 1)
        def _():
            xg.got_one()

        @pl.when(step == 2)
        def _():
            xg.got_two()

        @pl.when(step == 3)
        def _():
            xg.got_three()
            gg.start()

        xf = xs_ref[rows, :].astype(F32)
        n1_ref[rows, :] = (xf * rms_factor(xf) * gain1).astype(BF)
        proj = dot(n1_ref[rows, :], wqkv_ref[...]).astype(BF)
        qkv_ref[rows, :] = proj

    @pl.loop(0, 4)
    def _(turn):
        step = 3 - turn
        block = partner(me, step)
        rows = pl.ds(pl.multiple_of(block * toks, toks), toks)

        @pl.when(turn == 2)
        def _():
            gg.got_one()
            gg.got_two()

        for b in range(4):

            @pl.when(block == b)
            def _(b=b):
                upto = b * toks
                qrows = slice(upto, upto + toks)
                inside = lanes((toks, toks)) <= lax.broadcasted_iota(jnp.int32, (toks, toks), 0)
                for h in range(nq // HEAD_DIM):
                    g = h // group
                    q = qkv_ref[qrows, h * HEAD_DIM:(h + 1) * HEAD_DIM] * SCALE
                    kc = slice(nq + g * HEAD_DIM, nq + (g + 1) * HEAD_DIM)
                    vc = slice(nq + nk + g * HEAD_DIM, nq + nk + (g + 1) * HEAD_DIM)
                    near = jnp.where(inside, dot_t(q, qkv_ref[qrows, kc]), -1e30)
                    top = jnp.max(near, axis=-1, keepdims=True)
                    if b:
                        far = dot_t(q, qkv_ref[0:upto, kc])
                        top = jnp.maximum(top, jnp.max(far, axis=-1, keepdims=True))
                    near = jnp.exp(near - top)
                    total = jnp.sum(near, axis=-1, keepdims=True)
                    if b:
                        far = jnp.exp(far - top)
                        total = total + jnp.sum(far, axis=-1, keepdims=True)
                    inv = 1.0 / total
                    res = dot((near * inv).astype(BF), qkv_ref[qrows, vc])
                    if b:
                        res = res + dot((far * inv).astype(BF), qkv_ref[0:upto, vc])
                    attn_ref[qrows, h * HEAD_DIM:(h + 1) * HEAD_DIM] = res.astype(BF)
                    lse_ref[qrows, h:h + 1] = top + jnp.log(total)

        send_ref[step] = dot(attn_ref[rows, :], wo_ref[...]).astype(BF)

        @pl.when(step > 0)
        def _():
            send(send_ref.at[step], recv_ref.at[step], asem, step, block).start()

    mixed = x_ref[...].astype(F32) + send_ref[0].astype(F32)
    for step in (1, 2, 3):
        send(send_ref.at[step], recv_ref.at[step], asem, step, partner(me, step)).wait_recv()
        mixed = mixed + recv_ref[step].astype(F32)
    mixed_ref[...] = mixed
    n2 = (mixed * rms_factor(mixed) * gain_ref[1:2, :]).astype(BF)
    n2_ref[:, 0:n2.shape[1]] = n2
    logits = dot(n2, wr_ref[...])
    named = named_ref[...] > 0.0
    top = jnp.max(jnp.where(named, logits, -1e30), axis=-1, keepdims=True)
    weight = jnp.where(named, jnp.exp(jnp.minimum(logits - top, 0.0)), 0.0)
    gates = weight / jnp.sum(weight, axis=-1, keepdims=True)
    gate_ref[...] = gates
    n2_ref[:, n2.shape[1]:] = pack_two(gates, experts)
    gg.got_three()
    gg.finish()
    xg.finish()
    keep.wait()
    for step in (1, 2, 3):
        send(send_ref.at[step], recv_ref.at[step], asem, step, partner(me, step)).wait_send()


def front(nq, nk, experts, x, g, gains, named, wqkv, wo, wr):
    toks, d = x.shape
    length = 4 * toks
    sds = jax.ShapeDtypeStruct
    return pl.pallas_call(
        functools.partial(front_kernel, nq, nk, experts),
        name="front",
        out_shape=(
            sds((length, d), BF), sds((length, nq + 2 * nk), BF), sds((length, nq), BF), sds((length, 128), F32),
            sds((toks, d), F32), sds((toks, d + 128), BF), sds((toks, 128), F32), sds((length, d), BF),
        ),
        in_specs=[VM] * 7,
        out_specs=[VM] * 8,
        scratch_shapes=[
            pltpu.VMEM((length, d), BF), pltpu.VMEM((4, toks, d), BF), pltpu.VMEM((4, toks, d), BF),
            pltpu.SemaphoreType.DMA((2, 4)), pltpu.SemaphoreType.DMA((2, 4)), pltpu.SemaphoreType.DMA((2, 4)),
            pltpu.SemaphoreType.DMA,
        ],
        compiler_params=pltpu.CompilerParams(collective_id=1, has_side_effects=True, vmem_limit_bytes=56 * MIB),
        cost_estimate=pl.CostEstimate(flops=20 * 10**9, bytes_accessed=60 * 10**6, transcendentals=4 * 10**6),
    )(x, g, gains, named, wqkv, wo, wr)


def middle_kernel(
    experts, n2o_ref, gs_ref, gate_ref, mixed_ref, gain_ref, gu_hbm, wd_hbm, wr_ref,
    ggu_ref, gwd_ref, outp_ref, dmixed_ref, dproj_ref, grouter_ref,
    n2_ref, gu_ref, wd_ref, dpre_ref, hg_ref, send_ref, recv_ref, nsem, dsem, lsem,
):
    me = lax.axis_index("seq")
    toks, de = n2o_ref.shape
    d = de - 128
    ff = wd_ref.shape[0]
    fc = ff // experts
    load_gu = pltpu.make_async_copy(gu_hbm, gu_ref, lsem.at[0])
    load_wd = pltpu.make_async_copy(wd_hbm, wd_ref, lsem.at[1])
    load_gu.start()
    load_wd.start()
    greet(me)
    ng = Gather(me, n2o_ref, n2_ref, nsem)
    ng.start()
    load_gu.wait()
    load_wd.wait()

    @pl.loop(0, 4)
    def _(step):
        block = partner(me, step)
        rows = pl.ds(pl.multiple_of(block * toks, toks), toks)

        @pl.when(step == 0)
        def _():
            n2_ref[rows, :] = n2o_ref[...]

        @pl.when(step == 1)
        def _():
            ng.got_one()

        @pl.when(step == 2)
        def _():
            ng.got_two()

        @pl.when(step == 3)
        def _():
            ng.got_three()

        send_ref[step, :, d:] = jnp.zeros((toks, 128), BF)

        def one_expert(e, dgate):
            cols = pl.ds(pl.multiple_of(e * 2 * fc, 2 * fc), 2 * fc)
            hcols = pl.ds(pl.multiple_of(e * fc, fc), fc)
            pre = dot(n2_ref[rows, 0:d], gu_ref[:, cols])
            dh0 = dot_t(gs_ref[rows, :], wd_ref[hcols, :])
            packed = n2_ref[rows, d:].astype(F32)
            lane = lanes(packed.shape)
            mine = (lane == e) | (lane == e + experts)
            gate = jnp.sum(jnp.where(mine, packed, 0.0), axis=-1, keepdims=True)
            gp, up = pre[:, 0:fc], pre[:, fc:]
            sig = 1.0 / (1.0 + jnp.exp(-gp))
            act = gp * sig
            hid = (act * up).astype(BF).astype(F32)
            hg_ref[rows, hcols] = (gate * hid).astype(BF)
            dh = gate * dh0
            dpre_ref[rows, pl.ds(pl.multiple_of(e * 2 * fc, fc), fc)] = (
                dh * up * sig * (1.0 + gp * (1.0 - sig))).astype(BF)
            dpre_ref[rows, pl.ds(pl.multiple_of(e * 2 * fc + fc, fc), fc)] = (dh * act).astype(BF)
            return dgate + jnp.where(lane == e, jnp.sum(hid * dh0, axis=-1, keepdims=True), 0.0)

        dgate = lax.fori_loop(0, experts, one_expert, jnp.zeros((toks, 128), F32))
        send_ref[step, :, d:] = pack_two(dgate, experts)
        tile = 512

        @pl.loop(0, d // tile)
        def _(t):
            cols = pl.ds(pl.multiple_of(t * tile, tile), tile)
            send_ref[step, :, cols] = dot_t(dpre_ref[rows, :], gu_ref[cols, :]).astype(BF)

        @pl.when(step > 0)
        def _():
            send(send_ref.at[step], recv_ref.at[step], dsem, step, block).start()

        @pl.loop(0, d // tile)
        def _(t):
            cols = pl.ds(pl.multiple_of(t * tile, tile), tile)
            outp_ref[step, :, cols] = dot(hg_ref[rows, :], wd_ref[:, cols]).astype(BF)

    @pl.loop(0, d // 256)
    def _(t):
        cols = pl.ds(pl.multiple_of(t * 256, 256), 256)
        ggu_ref[cols, :] = t_dot(n2_ref[:, cols], dpre_ref[...]).astype(BF)

    @pl.loop(0, ff // 256)
    def _(t):
        cols = pl.ds(pl.multiple_of(t * 256, 256), 256)
        gwd_ref[cols, :] = t_dot(hg_ref[:, cols], gs_ref[...]).astype(BF)

    total = send_ref[0].astype(F32)
    for step in (1, 2, 3):
        send(send_ref.at[step], recv_ref.at[step], dsem, step, partner(me, step)).wait_recv()
        total = total + recv_ref[step].astype(F32)
    both = total[:, d:]
    lane = lanes(both.shape)
    dgate = jnp.where(lane < experts, both + pltpu.roll(both, 128 - experts, 1), 0.0)
    gates = gate_ref[...]
    dlog = (gates * (dgate - jnp.sum(gates * dgate, axis=-1, keepdims=True))).astype(BF)
    grouter_ref[...] = pack_two(t_dot(n2o_ref[:, 0:d], dlog), experts)
    dn = (total[:, 0:d] + dot_t(dlog, wr_ref[...])) * gain_ref[1:2, :]
    mixed = mixed_ref[...]
    r2 = rms_factor(mixed)
    own = gs_ref[pl.ds(pl.multiple_of(me * toks, toks), toks), :].astype(F32)
    dmixed = own + r2 * dn - mixed * (r2 * r2 * r2) * jnp.mean(dn * mixed, axis=-1, keepdims=True)
    dmixed_ref[...] = dmixed
    dproj_ref[...] = dmixed.astype(BF)
    ng.finish()
    for step in (1, 2, 3):
        send(send_ref.at[step], recv_ref.at[step], dsem, step, partner(me, step)).wait_send()


def middle(experts, n2o, gs, gates, mixed, gains, gu, wd, wr):
    toks, de = n2o.shape
    d = de - 128
    length = 4 * toks
    ff = wd.shape[0]
    sds = jax.ShapeDtypeStruct
    return pl.pallas_call(
        functools.partial(middle_kernel, experts),
        name="middle",
        out_shape=(
            sds((d, 2 * ff), BF), sds((ff, d), BF), sds((4, toks, d), BF), sds((toks, d), F32), sds((toks, d), BF),
            sds((d, 128), BF),
        ),
        in_specs=[VM] * 5 + [ANY] * 2 + [VM],
        out_specs=[VM] * 6,
        scratch_shapes=[
            pltpu.VMEM((length, de), BF), pltpu.VMEM((d, 2 * ff), BF), pltpu.VMEM((ff, d), BF),
            pltpu.VMEM((length, 2 * ff), BF), pltpu.VMEM((length, ff), BF),
            pltpu.VMEM((4, toks, de), BF), pltpu.VMEM((4, toks, de), BF),
            pltpu.SemaphoreType.DMA((2, 4)), pltpu.SemaphoreType.DMA((2, 4)), pltpu.SemaphoreType.DMA((2,)),
        ],
        compiler_params=pltpu.CompilerParams(collective_id=2, has_side_effects=True, vmem_limit_bytes=62 * MIB),
        cost_estimate=pl.CostEstimate(flops=60 * 10**9, bytes_accessed=80 * 10**6, transcendentals=4 * 10**6),
    )(n2o, gs, gates, mixed, gains, gu, wd, wr)


def back_kernel(
    nq, nk, x_ref, mixed_ref, dmixed_ref, dprojo_ref, gain_ref, n1_ref, qkv_ref, attn_ref, lse_ref, outp_ref,
    grouter_ref, wqkv_ref, wo_ref,
    out_ref, gin_ref, gqkv_ref, gwo_ref,
    dproj_ref, dattn_ref, dqkv_ref, dk_ref, dv_ref, send_ref, recv_ref, orecv_ref, psem, dsem, osem,
):
    me = lax.axis_index("seq")
    toks, d = x_ref.shape
    group = nq // nk
    greet(me)
    pg = Gather(me, dprojo_ref, dproj_ref, psem)
    pg.start()

    @pl.loop(0, 4)
    def _(step):
        block = partner(me, step)
        rows = pl.ds(pl.multiple_of(block * toks, toks), toks)

        @pl.when(step == 0)
        def _():
            dproj_ref[rows, :] = dprojo_ref[...]

        @pl.when(step == 1)
        def _():
            pg.got_one()

        @pl.when(step == 2)
        def _():
            pg.got_two()

        @pl.when(step == 3)
        def _():
            pg.got_three()

        dattn_ref[rows, :] = dot_t(dproj_ref[rows, :], wo_ref[...]).astype(BF)

    for step in (3, 2, 1):
        send(outp_ref.at[step], orecv_ref.at[step], osem, step, partner(me, step)).start()

    dk_ref[...] = jnp.zeros_like(dk_ref)
    dv_ref[...] = jnp.zeros_like(dv_ref)
    for b in range(4):
        upto = b * toks
        qrows = slice(upto, upto + toks)
        inside = lanes((toks, toks)) <= lax.broadcasted_iota(jnp.int32, (toks, toks), 0)
        for h in range(nq // HEAD_DIM):
            g = h // group
            hc = slice(h * HEAD_DIM, (h + 1) * HEAD_DIM)
            gc = slice(g * HEAD_DIM, (g + 1) * HEAD_DIM)
            q = qkv_ref[qrows, hc] * SCALE
            da = dattn_ref[qrows, hc]
            lse = lse_ref[qrows, h:h + 1]
            parts = ([slice(0, upto)] if b else []) + [qrows]
            probs, dprobs = [], []
            delta = 0.0
            for krows in parts:
                k = qkv_ref[krows, nq + g * HEAD_DIM: nq + (g + 1) * HEAD_DIM]
                v = qkv_ref[krows, nq + nk + g * HEAD_DIM: nq + nk + (g + 1) * HEAD_DIM]
                p = jnp.exp(dot_t(q, k) - lse)
                if krows is qrows:
                    p = jnp.where(inside, p, 0.0)
                dp = dot_t(da, v)
                delta = delta + jnp.sum(p * dp, axis=-1, keepdims=True)
                probs.append(p)
                dprobs.append(dp)
            dq = 0.0
            for krows, p, dp in zip(parts, probs, dprobs):
                k = qkv_ref[krows, nq + g * HEAD_DIM: nq + (g + 1) * HEAD_DIM]
                ds = (p * (dp - delta)).astype(BF)
                dq = dq + dot(ds, k)
                dk_ref[krows, gc] += t_dot(ds, q)
                dv_ref[krows, gc] += t_dot(p.astype(BF), da)
            dqkv_ref[qrows, hc] = (dq * SCALE).astype(BF)
    dqkv_ref[:, nq:nq + nk] = dk_ref[...].astype(BF)
    dqkv_ref[:, nq + nk:] = dv_ref[...].astype(BF)

    @pl.loop(0, 4)
    def _(turn):
        step = 3 - turn
        block = partner(me, step)
        rows = pl.ds(pl.multiple_of(block * toks, toks), toks)
        send_ref[step] = dot_t(dqkv_ref[rows, :], wqkv_ref[...]).astype(BF)

        @pl.when(step > 0)
        def _():
            send(send_ref.at[step], recv_ref.at[step], dsem, step, block).start()

    @pl.loop(0, d // 256)
    def _(t):
        cols = pl.ds(pl.multiple_of(t * 256, 256), 256)
        gqkv_ref[cols, 0:nq + 2 * nk] = t_dot(n1_ref[:, cols], dqkv_ref[...]).astype(BF)

    gqkv_ref[:, nq + 2 * nk:] = grouter_ref[...]

    @pl.loop(0, nq // 128)
    def _(t):
        cols = pl.ds(pl.multiple_of(t * 128, 128), 128)
        gwo_ref[cols, :] = t_dot(attn_ref[:, cols], dproj_ref[...]).astype(BF)

    out = mixed_ref[...] + outp_ref[0].astype(F32)
    for step in (1, 2, 3):
        send(outp_ref.at[step], orecv_ref.at[step], osem, step, partner(me, step)).wait_recv()
        out = out + orecv_ref[step].astype(F32)
    out_ref[...] = out.astype(BF)
    dn = send_ref[0].astype(F32)
    for step in (1, 2, 3):
        send(send_ref.at[step], recv_ref.at[step], dsem, step, partner(me, step)).wait_recv()
        dn = dn + recv_ref[step].astype(F32)
    dn = dn * gain_ref[0:1, :]
    xf = x_ref[...].astype(F32)
    r1 = rms_factor(xf)
    gin_ref[...] = (
        dmixed_ref[...] + r1 * dn - xf * (r1 * r1 * r1) * jnp.mean(dn * xf, axis=-1, keepdims=True)).astype(BF)
    pg.finish()
    for step in (1, 2, 3):
        send(send_ref.at[step], recv_ref.at[step], dsem, step, partner(me, step)).wait_send()
        send(outp_ref.at[step], orecv_ref.at[step], osem, step, partner(me, step)).wait_send()


def back(nq, nk, x, mixed, dmixed, dproj, gains, n1, qkv, attn, lse, outp, grouter, wqkv, wo):
    toks, d = x.shape
    length = 4 * toks
    sds = jax.ShapeDtypeStruct
    return pl.pallas_call(
        functools.partial(back_kernel, nq, nk),
        name="back",
        out_shape=(
            sds((toks, d), BF), sds((toks, d), BF), sds((d, nq + 2 * nk + 128), BF), sds((nq, d), BF),
        ),
        in_specs=[VM] * 13,
        out_specs=[VM] * 4,
        scratch_shapes=[
            pltpu.VMEM((length, d), BF), pltpu.VMEM((length, nq), BF), pltpu.VMEM((length, nq + 2 * nk), BF),
            pltpu.VMEM((length, nk), F32), pltpu.VMEM((length, nk), F32),
            pltpu.VMEM((4, toks, d), BF), pltpu.VMEM((4, toks, d), BF), pltpu.VMEM((4, toks, d), BF),
            pltpu.SemaphoreType.DMA((2, 4)), pltpu.SemaphoreType.DMA((2, 4)), pltpu.SemaphoreType.DMA((2, 4)),
        ],
        compiler_params=pltpu.CompilerParams(collective_id=3, has_side_effects=True, vmem_limit_bytes=62 * MIB),
        cost_estimate=pl.CostEstimate(flops=40 * 10**9, bytes_accessed=60 * 10**6, transcendentals=4 * 10**6),
    )(x, mixed, dmixed, dproj, gains, n1, qkv, attn, lse, outp, grouter, wqkv, wo)


def shards(x, cot, routes, gain_attn, w_query, w_key, w_value, w_out, gain_ffn, router, w_gate, w_up, w_down):
    n_seq = lax.axis_size("seq")
    n_fsdp = lax.axis_size("fsdp")
    rows, d = w_query.shape
    experts, ff_rows, _ = w_down.shape
    ff = w_gate.shape[2]
    fc = ff // n_seq

    extra = jnp.concatenate(
        [gain_attn[:, None], gain_ffn[:, None], router, jnp.zeros((rows, 128 - 2 - experts), BF)], axis=1
    )
    qkv = jnp.concatenate(
        [w_query.reshape(rows, n_seq, -1), w_key.reshape(rows, n_seq, -1), w_value.reshape(rows, n_seq, -1),
         jnp.broadcast_to(extra[:, None], (rows, n_seq, 128))], axis=2,
    )
    gu = jnp.stack([w_gate, w_up]).reshape(2, experts, rows, n_seq, fc).transpose(3, 2, 1, 0, 4)
    gu = gu.reshape(n_seq, rows, 2 * experts * fc)
    qkv = qkv.transpose(1, 0, 2)
    qkv = lax.all_to_all(qkv, "seq", split_axis=0, concat_axis=0, tiled=True)
    gu = lax.all_to_all(gu, "seq", split_axis=0, concat_axis=0, tiled=True)
    do = jnp.concatenate([w_down.reshape(experts * ff_rows, d), w_out], axis=0)
    qkv = lax.all_gather(qkv, "fsdp", axis=1).reshape(d, -1)
    do = lax.all_gather(do, "fsdp", axis=0)
    wo = do[:, experts * ff_rows:].reshape(-1, d)
    wd = do[:, : experts * ff_rows].reshape(n_fsdp, experts, ff_rows, d).transpose(1, 0, 2, 3).reshape(-1, d)
    gu = lax.all_gather(gu, "fsdp", axis=1).reshape(d, -1)

    nq, nk = w_query.shape[1] // n_seq, w_key.shape[1] // n_seq
    nqkv = nq + 2 * nk
    wqkv = qkv[:, :nqkv]
    gains = qkv[:, nqkv: nqkv + 8].T.astype(F32)
    wr = jnp.pad(qkv[:, nqkv + 2: nqkv + 2 + experts], ((0, 0), (0, 128 - experts)))
    hot = routes[0][:, :, None] == jnp.arange(128)[None, None, :]
    named = jnp.any(hot, axis=1).astype(F32)

    n1, proj, attn, lse, mixed, n2o, gates, gs = front(nq, nk, experts, x[0], cot[0], gains, named, wqkv, wo, wr)
    ggu, gwd, outp, dmixed, dproj, grouter = middle(experts, n2o, gs, gates, mixed, gains, gu, wd, wr)
    gwd = gwd.reshape(experts, n_fsdp, ff_rows, d).transpose(1, 0, 2, 3).reshape(-1, d)
    gwd = lax.psum_scatter(gwd, "fsdp", scatter_dimension=0, tiled=True)
    ggu = ggu.reshape(n_seq, n_fsdp, rows, -1).transpose(1, 0, 2, 3).reshape(n_fsdp * n_seq * rows, -1)
    ggu = lax.psum_scatter(ggu, "fsdp", scatter_dimension=0, tiled=True).reshape(n_seq, rows, -1)
    ggu = lax.all_to_all(ggu, "seq", split_axis=0, concat_axis=0, tiled=True)
    output, gin, gqkv, gwo = back(
        nq, nk, x[0], mixed, dmixed, dproj, gains, n1, proj, attn, lse, outp, grouter, wqkv, wo)
    gwo = lax.psum_scatter(gwo, "fsdp", scatter_dimension=0, tiled=True)
    gqkv = gqkv.reshape(n_seq, n_fsdp, rows, -1).transpose(1, 0, 2, 3).reshape(n_fsdp * n_seq * rows, -1)
    gqkv = lax.psum_scatter(gqkv, "fsdp", scatter_dimension=0, tiled=True).reshape(n_seq, rows, -1)
    gqkv = lax.all_to_all(gqkv, "seq", split_axis=0, concat_axis=0, tiled=True)

    gqkv = gqkv.astype(F32)
    g_query = gqkv[:, :, :nq].transpose(1, 0, 2).reshape(rows, -1)
    g_key = gqkv[:, :, nq: nq + nk].transpose(1, 0, 2).reshape(rows, -1)
    g_value = gqkv[:, :, nq + nk: nqkv].transpose(1, 0, 2).reshape(rows, -1)
    g_router = jnp.sum(gqkv[:, :, nqkv: nqkv + experts] + gqkv[:, :, nqkv + experts: nqkv + 2 * experts], axis=0)
    ggu = ggu.astype(F32).reshape(n_seq, rows, experts, 2, fc).transpose(3, 2, 1, 0, 4).reshape(2, experts, rows, ff)
    g_gate, g_up = ggu[0], ggu[1]
    g_gain_one = (
        jnp.sum(w_query.astype(F32) * g_query, axis=1) + jnp.sum(w_key.astype(F32) * g_key, axis=1)
        + jnp.sum(w_value.astype(F32) * g_value, axis=1)
    ) / gain_attn.astype(F32)
    g_gain_two = (
        jnp.sum(w_gate.astype(F32) * g_gate + w_up.astype(F32) * g_up, axis=(0, 2))
        + jnp.sum(router.astype(F32) * g_router, axis=1)
    ) / gain_ffn.astype(F32)
    return (
        output[None], gin[None], g_gain_one, g_query, g_key, g_value, gwo.astype(F32), g_gain_two, g_router,
        g_gate, g_up, gwd.astype(F32).reshape(experts, ff_rows, d),
    )


def solution(mesh):
    tok = P("fsdp", "seq", None)
    vec = P(("seq", "fsdp"))
    mat = P(("seq", "fsdp"), None)
    exp = P(None, ("seq", "fsdp"), None)
    return jax.shard_map(
        shards,
        mesh=mesh,
        in_specs=(tok, tok, tok, vec, mat, mat, mat, mat, vec, mat, exp, exp, exp),
        out_specs=(tok, tok, vec, mat, mat, mat, mat, vec, mat, exp, exp, exp),
        check_vma=False,
    )
```

time: 809 us -> 602 us (0.74)
  Pallas kernels: 0 us -> 286 us
  waiting for transfers between devices: 454 us -> 211 us
  matrix products: 158 us -> 0 us
  other arithmetic: 62.2 us -> 11.1 us
  local copies, waits for them, and re-layouts: 60 us -> 40 us
  blocking collectives: 40.8 us -> 24.9 us
    pallas_call x0 -> x3, Pallas kernels: none -> 286 us  [the longest x1 105 us: back(): pl.pallas_call(functools.partial(back_kernel, nq, nk), name='back', out_s...]
    reduce_scatter x4 -> x0, waiting for transfers between devices: 169 us -> none  [the longest x1 46.2 us: shards(): lax.psum_scatter(dn2p, 'seq', scatter_dimension=0, tiled=True).astype(F32)]
    dot_general x21 -> x0, matrix products: 158 us -> none  [the longest x5 39.5 us: dot_t(): lax.dot_general(a, b, (((1,), (1,)), ((), ())), preferred_element_type=F32)]
    all_gather x4 -> x0, waiting for transfers between devices: 108 us -> none  [the longest x1 41.2 us: shards(): xs = lax.all_gather(x[0], 'seq', axis=0, tiled=True)]
    reduce_scatter x1, waiting for transfers between devices: 0.02 us -> 67.5 us  [shards(): lax.psum_scatter(ggu, 'fsdp', scatter_dimension=0, tiled=True)]
    all_gather x1, waiting for transfers between devices: 58.7 us -> 0.02 us  [shards(): gu = lax.all_gather(gu, 'fsdp', axis=1).reshape(d, -1)]
    all_gather x1, waiting for transfers between devices: 11.7 us -> 42.8 us  [shards(): do = lax.all_gather(do, 'fsdp', axis=0)]
    convert_element_type x5 -> x2, other arithmetic: 22.8 us -> 1.72 us  [the longest x1 1.05 us: shards(): gains = qkv[:, nqkv:nqkv + 8].T.astype(F32)]
  transfers between devices with their start and end apart: 18 -> 9, of which waited for: 15 -> 6; matrix products, arithmetic and copies ran while one was open for 29% -> 6% of each run, Pallas kernels for 0% -> 17%
where the time goes in v2:
time: 602 us; the launch traced here: 597 us
  Pallas kernels  286 us (48%)
  waiting for transfers between devices  211 us (35%)
  local copies, waits for them, and re-layouts  40 us (7%)
  blocking collectives  24.9 us (4%)
  between operations  14.8 us (2%)
  other arithmetic  11.1 us (2%)
  starting transfers between devices  8.19 us (1%)
    pallas_call x1, Pallas kernels, back(): pl.pallas_call(functools.partial(back_kernel, nq, nk), name='back', out_s...  105 us
    pallas_call x1, Pallas kernels, front(): pl.pallas_call(functools.partial(front_kernel, nq, nk, experts), name='fr...  99.9 us
    pallas_call x1, Pallas kernels, middle(): pl.pallas_call(functools.partial(middle_kernel, experts), name='middle',...  82 us
    reduce_scatter x1, waiting for transfers between devices, shards(): lax.psum_scatter(ggu, 'fsdp', scatter_dimension=0, tiled=True)  67.5 us
    all_gather x1, waiting for transfers between devices, shards(): do = lax.all_gather(do, 'fsdp', axis=0)  42.8 us
    reduce_scatter x1, waiting for transfers between devices, shards(): gwd = lax.psum_scatter(gwd, 'fsdp', scatter_dimension=0, tiled=True)  34.9 us
    reduce_scatter x1, waiting for transfers between devices, shards(): gwo = lax.psum_scatter(gwo, 'fsdp', scatter_dimension=0, tiled=True)  30.4 us
    reduce_scatter x1, waiting for transfers between devices, shards(): lax.psum_scatter(gqkv, 'fsdp', scatter_dimension=0, tiled=True)  22.8 us
  transfers between devices with their start and end apart: 9, of which 6 were waited for; matrix products, arithmetic and copies ran while one was open for 6% of the time, Pallas kernels for 17%

profile of v2, /device:TPU:0, one launch (start us, length us, event | category | flops | bytes accessed | tf_op | source)
XLA Modules:
  0.0 596.8 jit_solution(10019327492908384231)
XLA Ops:
  7.3 1.0 copy.128
  8.3 0.8 copy.94
  9.0 0.8 copy.95
  9.8 0.8 copy.96
  10.6 0.8 copy_bitcast_fusion.3
  11.4 0.1 pad.16.clone
  11.5 0.1 maximum_maximum_fusion
  11.6 11.4 %all_to_all.20 = bf16[4,48,768]{2,1,0:T(8,128)(2,1)} all-to-all(bf16[4,48,768]{2,1,0:T(8,128)(2,1)S(1)} %maximum_bitcast_fusion.1), channel_id=1, replica_groups=mesh['seq'=4,'fsdp'=8] {'seq'}, dimensions={0} | all-to-all | bytes 589824 | tf_op jit(solution)/shard_map/all_to_all | solution.py:536
  23.1 0.0 all-gather.9.cloned.1.call-start
  23.1 1.7 pad_maximum_fusion
  24.9 0.0 all-gather.11.cloned.1.call-start
  24.9 0.3 stack.10
  25.2 0.3 stack.9
  25.5 0.6 maximum_bitcast_fusion
  26.1 0.8 copy.101
  26.9 0.6 reshape.115
  27.5 13.5 %all_to_all.21 = bf16[4,48,2048]{2,1,0:T(8,128)(2,1)} all-to-all(bf16[4,48,2048]{2,1,0:T(8,128)(2,1)S(1)} %reshape.115), channel_id=1, replica_groups=mesh['seq'=4,'fsdp'=8] {'seq'}, dimensions={0} | all-to-all | bytes 1572864 | tf_op jit(solution)/shard_map/all_to_all | solution.py:537
  41.1 0.1 fusion
  41.2 0.7 convert_element_type.44.named_ref
  41.9 12.4 %all-gather.7.cloned.1.call-done = bf16[4,384,768]{2,1,0:T(8,128)(2,1)} async-done(((bf16[4,48,768]{2,1,0:T(8,128)(2,1)}), bf16[4,384,768]{2,1,0:T(8,128)(2,1)}) %all-gather.7.cloned.1.call-update) | async-done | bytes 2359312 | tf_op jit(solution)/shard_map/all_gather | solution.py:539
  54.3 3.1 slice.51.wqkv_ref
  57.4 1.2 slice.53
  58.6 1.0 convert_bitcast_fusion
  59.6 0.9 copy.100.gain_ref
  60.5 0.8 pad.4.wr_ref
  61.3 42.8 %all-gather.9.cloned.1.call-done = bf16[1408,1536]{1,0:T(8,128)(2,1)} async-done(((bf16[176,1536]{1,0:T(8,128)(2,1)}), bf16[1408,1536]{1,0:T(8,128)(2,1)}) %all-gather.9.cloned.1.call-update) | async-done | bytes 4325392 | tf_op jit(solution)/shard_map/all_gather | solution.py:540
  104.1 2.4 slice.52
  106.5 2.1 slice.54
  108.6 2.1 copy.102
  110.6 99.9 %front.1 = (bf16[1024,1536]{1,0:T(8,128)(2,1)}, bf16[1024,640]{1,0:T(8,128)(2,1)}, bf16[1024,384]{1,0:T(8,128)(2,1)}, f32[1024,128]{1,0:T(8,128)}, f32[256,1536]...) custom-call(bf16[256,1536]{1,0:T(8,128)(2,1)} %bitcast.100, ...), custom_call_target="tpu_custom_call" | custom-call | flops 20000000000 | bytes 60000000 | tf_op jit(solution)/shard_map/front/pallas_call | solution.py:218
  210.6 82.0 %middle.1 = (bf16[1536,2048]{1,0:T(8,128)(2,1)}, bf16[1024,1536]{1,0:T(8,128)(2,1)}, bf16[4,256,1536]{2,1,0:T(8,128)(2,1)}, f32[256,1536]{1,0:T(8,128)}, bf16[25...) custom-call(bf16[256,1664]{1,0:T(8,128)(2,1)} %get-tuple-element.31.n2o_ref, bf16[1024,1536]{1,0:T(8,128)(2,1)} %get-tuple-element.32.gs_ref, ...), custom_call_target="tpu_custom_call" | custom-call | flops 60000002048 | bytes 80000000 | tf_op jit(solution)/shard_map/middle/pallas_call | solution.py:356
  292.6 104.5 %back.1 = (bf16[256,1536]{1,0:T(8,128)(2,1)}, bf16[256,1536]{1,0:T(8,128)(2,1)}, bf16[1536,768]{1,0:T(8,128)(2,1)}, bf16[384,1536]{1,0:T(8,128)(2,1)}) custom-call(bf16[256,1536]{1,0:T(8,128)(2,1)} %bitcast.101, f32[256,1536]{1,0:T(8,128)} %get-tuple-element.30.mixed_ref, f32[256,1536]{1,0:T(8,128)} %get-tuple-element.34.dmixed_ref, ...), custom_call_target="tpu_custom_call" | custom-call | flops 40000000000 | bytes 60000000 | tf_op jit(solution)/shard_map/back/pallas_call | solution.py:499
  397.1 3.3 copy.105
  400.4 0.5 reduce-scatter.7.cloned.1.call-update
  401.0 6.5 %copy.109 = bf16[4,8,48,2048]{3,2,0,1:T(8,128)(2,1)} copy(bf16[4,8,48,2048]{3,2,1,0:T(8,128)(2,1)} %bitcast.73) | data formatting | bytes 12582912 | tf_op jit(solution)/shard_map/reshape | solution.py:557
  407.7 1.8 copy-done.2
  409.5 1.9 copy.113
  411.4 22.8 %reduce-scatter.5.cloned.1.call-done = bf16[192,768]{1,0:T(8,128)(2,1)} async-done(((bf16[1536,768]{1,0:T(8,128)(2,1)}), bf16[192,768]{1,0:T(8,128)(2,1)}) %reduce-scatter.5.cloned.1.call-update) | async-done | bytes 294928 | tf_op jit(solution)/shard_map/reduce_scatter | solution.py:564
  434.2 4.0 all-to-all-start.2
  438.2 0.1 copy.112
  438.3 30.4 %reduce-scatter.7.cloned.1.call-done = bf16[48,1536]{1,0:T(8,128)(2,1)} async-done(((bf16[384,1536]{1,0:T(8,128)(2,1)}), bf16[48,1536]{1,0:T(8,128)(2,1)}) %reduce-scatter.7.cloned.1.call-update) | async-done | bytes 147472 | tf_op jit(solution)/shard_map/reduce_scatter | solution.py:562
  468.7 1.6 convert_element_type.50
  470.4 0.1 fusion.1
  470.6 0.8 multiply_reduce_fusion.2
  471.3 67.5 %reduce-scatter.9.cloned.1.call-done = bf16[192,2048]{1,0:T(8,128)(2,1)} async-done(((bf16[1536,2048]{1,0:T(8,128)(2,1)}), bf16[192,2048]{1,0:T(8,128)(2,1)}) %reduce-scatter.9.cloned.1.call-update) | async-done | bytes 786448 | tf_op jit(solution)/shard_map/reduce_scatter | solution.py:558
  538.8 3.9 all-to-all-start.3
  542.7 0.1 multiply_reduce_fusion.3
  542.8 0.7 copy.114
  543.5 0.1 multiply_reduce_fusion
  543.7 0.8 multiply_reduce_fusion.1
  544.4 0.5 convert_divide_fusion.1
  544.9 34.9 %reduce-scatter.11.cloned.1.call-done = bf16[128,1536]{1,0:T(8,128)(2,1)} async-done(((bf16[1024,1536]{1,0:T(8,128)(2,1)}), bf16[128,1536]{1,0:T(8,128)(2,1)}) %reduce-scatter.11.cloned.1.call-update) | async-done | bytes 393232 | tf_op jit(solution)/shard_map/reduce_scatter | solution.py:556
  579.8 2.0 convert.4
  581.8 1.6 reshape.135
  583.3 1.2 fusion.2
  584.6 0.5 copy.110
  585.1 0.4 squeeze.15
  585.5 0.5 copy.111
  586.1 0.4 squeeze.16
  586.5 0.3 add_reduce_fusion
  586.8 0.5 convert_divide_fusion
  587.4 0.5 copy-done.8
  587.9 0.9 copy.131
  588.8 0.9 copy.132
  (53 shorter events, 0.6 us)
Async XLA Ops:
  7.2 15.9 %copy-start.10 = (bf16[4,32,1536]{2,1,0:T(8,128)(2,1)S(1)}, bf16[4,32,1536]{2,1,0:T(8,128)(2,1)}, u32[]{:S(2)}) copy-start(bf16[4,32,1536]{2,1,0:T(8,128)(2,1)} %param.25) | copy-start | bytes 1179652
  7.2 17.7 %copy-start.3 = (bf16[4,48,1024]{2,1,0:T(8,128)(2,1)S(1)}, bf16[4,48,1024]{2,1,0:T(8,128)(2,1)}, u32[]{:S(2)}) copy-start(bf16[4,48,1024]{2,1,0:T(8,128)(2,1)} %param.24) | copy-start | bytes 1179652
  7.2 18.0 %copy-start.4 = (bf16[4,48,1024]{2,1,0:T(8,128)(2,1)S(1)}, bf16[4,48,1024]{2,1,0:T(8,128)(2,1)}, u32[]{:S(2)}) copy-start(bf16[4,48,1024]{2,1,0:T(8,128)(2,1)} %param.23) | copy-start | bytes 1179652
  7.2 47.1 %all-gather.7.cloned.1.call-start = ((), (), s32[]{:S(2)}) async-start(), calls=%async_computation.12 | async-start | bytes 2654208 | tf_op jit(solution)/shard_map/all_gather | solution.py:539
  23.1 81.1 %all-gather.9.cloned.1.call-start = ((), (), s32[]{:S(2)}) async-start(), calls=%async_computation.13 | async-start | bytes 4866048 | tf_op jit(solution)/shard_map/all_gather | solution.py:540
  24.9 185.7 %all-gather.11.cloned.1.call-start = ((), (), s32[]{:S(2)}) async-start(), calls=%async_computation.14 | async-start | bytes 7077888 | tf_op jit(solution)/shard_map/all_gather | solution.py:543
  26.9 14.2 %copy-start.14 = (s32[1,256,2]{1,2,0:T(2,128)S(1)}, s32[1,256,2]{1,2,0:T(2,128)}, u32[]{:S(2)}) copy-start(s32[1,256,2]{1,2,0:T(2,128)} %param.15) | copy-start | bytes 6148
  41.0 393.2 %reduce-scatter.5.cloned.1.call-start = ((), (), s32[]{:S(2)}) async-start(), calls=%async_computation.8 | async-start | bytes 2654208 | tf_op jit(solution)/shard_map/reduce_scatter | solution.py:564
  400.4 68.3 %reduce-scatter.7.cloned.1.call-start = ((), (), s32[]{:S(2)}) async-start(), calls=%async_computation.9 | async-start | bytes 1327104 | tf_op jit(solution)/shard_map/reduce_scatter | solution.py:562
  401.0 137.8 %reduce-scatter.9.cloned.1.call-start = ((), (), s32[]{:S(2)}) async-start(), calls=%async_computation.10 | async-start | bytes 7077888 | tf_op jit(solution)/shard_map/reduce_scatter | solution.py:558
  407.6 1.9 copy-start.2
  407.6 172.2 %reduce-scatter.11.cloned.1.call-start = ((), (), s32[]{:S(2)}) async-start(), calls=%async_computation.11 | async-start | bytes 3538944 | tf_op jit(solution)/shard_map/reduce_scatter | solution.py:556
  411.3 26.9 %copy-start.13 = (bf16[48,4]{0,1:T(4,128)(2,1)S(1)}, bf16[48,4]{0,1:T(4,128)(2,1)}, u32[]{:S(2)}) copy-start(bf16[48,4]{0,1:T(4,128)(2,1)} %param.22) | copy-start | bytes 1156
  411.3 59.2 %copy-start.11 = (bf16[48,512]{1,0:T(8,128)(2,1)S(1)}, bf16[48,512]{1,0:T(8,128)(2,1)}, u32[]{:S(2)}) copy-start(bf16[48,512]{1,0:T(8,128)(2,1)} %param.18) | copy-start | bytes 147460
  434.2 36.2 %all-to-all-start.2 = ((bf16[4,48,768]{2,1,0:T(8,128)(2,1)}), bf16[4,48,768]{2,1,0:T(8,128)(2,1)S(1)}, u32[]{:S(2)}, u32[]{:S(2)}) async-start(bf16[4,48,768]{2,1,0:T(8,128)(2,1)} %bitcast.94), calls=%async_computation.3 | async-start | bytes 589824 | tf_op jit(solution)/shard_map/all_to_all | solution.py:565
  470.4 73.2 %copy-start.9 = (bf16[48,1536]{1,0:T(8,128)(2,1)S(1)}, bf16[48,1536]{1,0:T(8,128)(2,1)}, u32[]{:S(2)}) copy-start(bf16[48,1536]{1,0:T(8,128)(2,1)} %param.17) | copy-start | bytes 442372
  470.4 73.3 %copy-start.12 = (bf16[48,512]{1,0:T(8,128)(2,1)S(1)}, bf16[48,512]{1,0:T(8,128)(2,1)}, u32[]{:S(2)}) copy-start(bf16[48,512]{1,0:T(8,128)(2,1)} %param.19) | copy-start | bytes 147460
  470.4 74.0 %copy-start.15 = (bf16[48]{0:T(256)(128)(2,1)S(1)}, bf16[48]{0:T(256)(128)(2,1)}, u32[]{:S(2)}) copy-start(bf16[48]{0:T(256)(128)(2,1)} %param.16) | copy-start | bytes 292
  538.8 43.0 %all-to-all-start.3 = ((bf16[4,48,2048]{2,1,0:T(8,128)(2,1)}), bf16[4,48,2048]{2,1,0:T(8,128)(2,1)S(1)}, u32[]{:S(2)}, u32[]{:S(2)}) async-start(bf16[4,48,2048]{2,1,0:T(8,128)(2,1)} %bitcast.89), calls=%async_computation.6 | async-start | bytes 1572864 | tf_op jit(solution)/shard_map/all_to_all | solution.py:559
  543.5 41.1 %copy-start.6 = (f32[4,6,8,384]{3,2,0,1:T(8,128)}, f32[4,6,8,384]{3,2,0,1:T(8,128)S(1)}, u32[]{:S(2)}) copy-start(f32[4,6,8,384]{3,2,0,1:T(8,128)S(1)} %copy.118) | copy-start | bytes 884740
  585.1 1.4 copy-start.5
  585.5 1.3 copy-start
  586.0 0.8 copy-start.16
  586.5 3.2 copy-start.1
  586.5 1.4 copy-start.8
  586.5 2.3 copy-start.7
Sparse Core Ops, SparseCore 0:
  23.2 31.0 all-gather.6
  56.5 47.5 all-gather.8
  105.7 63.4 all-gather.10
  400.5 33.6 reduce-scatter.4
  436.3 32.3 reduce-scatter.6
  470.9 67.8 reduce-scatter.8
  541.1 38.6 reduce-scatter.10

commit v3 on v2

v3 whole, which is shorter than its diff:
```python
import functools

import jax
import jax.numpy as jnp
from jax import lax
from jax.experimental import pallas as pl
from jax.experimental.pallas import tpu as pltpu
from jax.sharding import PartitionSpec as P

HEAD_DIM = 64
EPS = 1e-06
SCALE = HEAD_DIM ** (-0.5)
BF = jnp.bfloat16
F32 = jnp.float32
MESH = pl.DeviceIdType.MESH
ANY = pl.BlockSpec(memory_space=pl.ANY)
VM = pl.BlockSpec(memory_space=pltpu.VMEM)
MIB = 2**20


def dot(a, b):
    return jnp.dot(a, b, preferred_element_type=F32)


def dot_t(a, b):
    return lax.dot_general(a, b, (((1,), (1,)), ((), ())), preferred_element_type=F32)


def t_dot(a, b):
    return lax.dot_general(a, b, (((0,), (0,)), ((), ())), preferred_element_type=F32)


def rms_factor(rows):
    return lax.rsqrt(jnp.mean(rows * rows, axis=-1, keepdims=True) + EPS)


def partner(me, step):
    return ((me // 2 + step // 2) % 2) * 2 + (me % 2 + step % 2) % 2


def send(src, dst, sems, slot, peer):
    return pltpu.make_async_remote_copy(
        src_ref=src, dst_ref=dst, send_sem=sems.at[0, slot], recv_sem=sems.at[1, slot],
        device_id={"seq": peer}, device_id_type=MESH,
    )


def greet(me, others):
    barrier = pltpu.get_barrier_semaphore()
    for step in (1, 2, 3):
        pl.semaphore_signal(barrier, inc=1, device_id={"seq": partner(me, step)}, device_id_type=MESH)
    pl.semaphore_wait(barrier, 3 + others)


class Gather:
    def __init__(self, me, own, buf, sems, base=0):
        rows = own.shape[0]
        half = rows // 2
        one, two = partner(me, 1), partner(me, 2)

        def part(owner, start, size):
            return buf.at[pl.ds(pl.multiple_of(owner * rows + start, half), size)]

        mine = part(me, 0, rows)
        self.first = send(own, mine, sems, base, one)
        self.second = send(own, mine, sems, base + 1, two)
        onward = part(one, 0, half)
        self.third = send(onward, onward, sems, base + 2, two)
        onward = part(two, half, half)
        self.fourth = send(onward, onward, sems, base + 3, one)

    def start(self):
        self.first.start()
        self.second.start()

    def got_one(self):
        self.first.wait_recv()
        self.third.start()

    def got_two(self):
        self.second.wait_recv()
        self.fourth.start()

    def got_three(self):
        self.third.wait_recv()
        self.fourth.wait_recv()

    def finish(self):
        for copy in (self.first, self.second, self.third, self.fourth):
            copy.wait_send()


def lanes(shape):
    return lax.broadcasted_iota(jnp.int32, shape, len(shape) - 1)


def pack_two(value, experts):
    high = value.astype(BF).astype(F32)
    low = value - high
    return jnp.where(lanes(value.shape) < experts, high, pltpu.roll(low, experts, 1)).astype(BF)


class Line:
    def __init__(self, region, sems):
        me = lax.axis_index("fsdp")
        self.last = lax.axis_size("fsdp") // 2 - 1
        self.z, self.core = me // 2, me % 2
        self.region, self.sems = region, sems

    def copy(self, slot, plane, core, target):
        part = self.region(plane * 2 + core)
        return pltpu.make_async_remote_copy(
            src_ref=part, dst_ref=part, send_sem=self.sems.at[0, slot], recv_sem=self.sems.at[1, slot],
            device_id={"fsdp": target}, device_id_type=MESH,
        )

    def up(self, hop):
        return self.copy(hop, self.z - hop, self.core, (self.z + 1) * 2 + self.core)

    def from_below(self, hop):
        return self.copy(hop, self.z - 1 - hop, self.core, self.z * 2 + self.core)

    def down(self, hop):
        return self.copy(3 + hop, self.z + hop, self.core, (self.z - 1) * 2 + self.core)

    def from_above(self, hop):
        return self.copy(3 + hop, self.z + 1 + hop, self.core, self.z * 2 + self.core)

    def across(self, plane):
        return self.copy(6 + plane, plane, self.core, self.z * 2 + 1 - self.core)

    def from_across(self, plane):
        return self.copy(6 + plane, plane, 1 - self.core, self.z * 2 + self.core)

    def start(self):
        pl.when(self.z < self.last)(lambda: self.up(0).start())
        pl.when(self.z > 0)(lambda: self.down(0).start())
        self.across(self.z).start()

    def step(self, hop):
        @pl.when(self.z > hop)
        def _():
            self.from_below(hop).wait_recv()
            if hop < 2:
                pl.when(self.z < self.last)(lambda: self.up(hop + 1).start())
            self.across(self.z - 1 - hop).start()

        @pl.when(self.z + hop < self.last)
        def _():
            self.from_above(hop).wait_recv()
            if hop < 2:
                pl.when(self.z > 0)(lambda: self.down(hop + 1).start())
            self.across(self.z + 1 + hop).start()

    def land(self):
        for plane in range(4):
            self.from_across(plane).wait_recv()

    def finish(self):
        for hop in range(3):
            pl.when((self.z >= hop) & (self.z < self.last))(lambda hop=hop: self.up(hop).wait_send())
            pl.when((self.z + hop <= self.last) & (self.z > 0))(lambda hop=hop: self.down(hop).wait_send())
        for plane in range(4):
            self.across(plane).wait_send()


def greet_line():
    me = lax.axis_index("fsdp")
    last = lax.axis_size("fsdp") // 2 - 1
    z, core = me // 2, me % 2
    barrier = pltpu.get_barrier_semaphore()

    @pl.when(z < last)
    def _():
        pl.semaphore_signal(barrier, inc=1, device_id={"fsdp": me + 2}, device_id_type=MESH)

    @pl.when(z > 0)
    def _():
        pl.semaphore_signal(barrier, inc=1, device_id={"fsdp": me - 2}, device_id_type=MESH)

    pl.semaphore_signal(barrier, inc=1, device_id={"fsdp": z * 2 + 1 - core}, device_id_type=MESH)
    return 1 + jnp.minimum(z, 1) + jnp.minimum(last - z, 1)


class Spread:
    def __init__(self, me, own, buf, shard, sems, local):
        self.copies = [
            send(own.at[partner(me, step)], buf.at[me, shard], sems, step, partner(me, step)) for step in (3, 2, 1)
        ]
        self.local = pltpu.make_async_copy(own.at[me], buf.at[me, shard], local)

    def start(self):
        self.local.start()
        for copy in self.copies:
            copy.start()

    def got(self):
        self.local.wait()
        for copy in self.copies:
            copy.wait_recv()

    def finish(self):
        for copy in self.copies:
            copy.wait_send()


def front_kernel(nq, nk, experts, inside, *refs):
    if inside:
        (x_ref, g_ref, named_ref, qkvo_ref, guo_ref, wdo_ref, woo_ref,
         n1_ref, qkv_ref, attn_ref, lse_ref, mixed_ref, n2_ref, gate_ref, gs_ref, gain_ref, ext_ref, wqkv_ref, wo_ref,
         gu_ref, wd_ref,
         xs_ref, send_ref, recv_ref, xsem, gsem, asem, lsem, qw_ref, spread_sem, line_sem) = refs
    else:
        (x_ref, g_ref, named_ref, wqkv_ref, wo_ref,
         n1_ref, qkv_ref, attn_ref, lse_ref, mixed_ref, n2_ref, gate_ref, gs_ref, gain_ref, ext_ref,
         xs_ref, send_ref, recv_ref, xsem, gsem, asem, lsem) = refs
    me = lax.axis_index("seq")
    toks, d = x_ref.shape
    group = nq // nk
    nqkv = nq + 2 * nk
    xg = Gather(me, x_ref, xs_ref, xsem)
    gg = Gather(me, g_ref, gs_ref, gsem)
    keep = pltpu.make_async_copy(g_ref, gs_ref.at[pl.ds(pl.multiple_of(me * toks, toks), toks)], lsem.at[0])
    keep.start()
    if inside:
        shard = lax.axis_index("fsdp")
        rows = woo_ref.shape[0]
        greet(me, greet_line())
        qkv_line = Line(lambda f: qw_ref.at[:, f], line_sem.at[0])
        wo_line = Line(lambda f: wo_ref.at[pl.ds(pl.multiple_of(f * rows, 16), rows)], line_sem.at[1])
        wd_line = Line(lambda f: wd_ref.at[:, f], line_sem.at[2])
        gu_line = Line(lambda f: gu_ref.at[:, f], line_sem.at[3])
        qkv_spread = Spread(me, qkvo_ref, qw_ref, shard, spread_sem.at[0], lsem.at[1])
        gu_spread = Spread(me, guo_ref, gu_ref, shard, spread_sem.at[1], lsem.at[2])
        place_wo = pltpu.make_async_copy(woo_ref, wo_line.region(shard), lsem.at[3])
        place_wd = pltpu.make_async_copy(wdo_ref, wd_line.region(shard), lsem.at[4])
        qkv_spread.start()
        place_wo.start()
        place_wd.start()
        xg.start()
        gu_spread.start()
        place_wo.wait()
        place_wd.wait()
        qkv_spread.got()
        qkv_line.start()
        wd_line.start()
        wo_line.start()
        xs_ref[pl.ds(pl.multiple_of(me * toks, toks), toks), :] = x_ref[...]
        qkv_line.step(0)
        gu_spread.got()
        gu_line.start()
        qkv_line.step(1)
        xg.got_one()
        xg.got_two()
        wd_line.step(0)
        wo_line.step(0)
        qkv_line.step(2)
        wo_line.step(1)
        wo_line.step(2)
        wd_line.step(1)
        xg.got_three()
        gg.start()
        qkv_line.land()
        for s in range(4):
            for f in range(8):
                wqkv_ref[s * 8 * rows + f * rows: s * 8 * rows + (f + 1) * rows, :] = qw_ref[s, f]
        wo_line.land()
    else:
        greet(me, 0)
        xg.start()
        xs_ref[pl.ds(pl.multiple_of(me * toks, toks), toks), :] = x_ref[...]
        xg.got_one()
        xg.got_two()
        xg.got_three()
        gg.start()
    ext = wqkv_ref[:, nqkv:]
    ext_ref[...] = ext
    gain_ref[...] = ext.astype(F32).T[experts:experts + 2, :]
    gain1 = gain_ref[0:1, :]

    @pl.loop(0, 4)
    def _(block):
        rows = pl.ds(pl.multiple_of(block * toks, toks), toks)
        xf = xs_ref[rows, :].astype(F32)
        n1_ref[rows, :] = (xf * rms_factor(xf) * gain1).astype(BF)
        proj = dot(n1_ref[rows, :], wqkv_ref[:, 0:nqkv]).astype(BF)
        qkv_ref[rows, :] = proj

    if inside:
        wd_line.step(2)
        gu_line.step(0)

    @pl.loop(0, 4)
    def _(turn):
        step = 3 - turn
        block = partner(me, step)
        rows = pl.ds(pl.multiple_of(block * toks, toks), toks)

        @pl.when(turn == 2)
        def _():
            gg.got_one()
            gg.got_two()
            if inside:
                gu_line.step(1)

        for b in range(4):

            @pl.when(block == b)
            def _(b=b):
                upto = b * toks
                qrows = slice(upto, upto + toks)
                inside = lanes((toks, toks)) <= lax.broadcasted_iota(jnp.int32, (toks, toks), 0)
                for h in range(nq // HEAD_DIM):
                    g = h // group
                    q = qkv_ref[qrows, h * HEAD_DIM:(h + 1) * HEAD_DIM] * SCALE
                    kc = slice(nq + g * HEAD_DIM, nq + (g + 1) * HEAD_DIM)
                    vc = slice(nq + nk + g * HEAD_DIM, nq + nk + (g + 1) * HEAD_DIM)
                    near = jnp.where(inside, dot_t(q, qkv_ref[qrows, kc]), -1e30)
                    top = jnp.max(near, axis=-1, keepdims=True)
                    if b:
                        far = dot_t(q, qkv_ref[0:upto, kc])
                        top = jnp.maximum(top, jnp.max(far, axis=-1, keepdims=True))
                    near = jnp.exp(near - top)
                    total = jnp.sum(near, axis=-1, keepdims=True)
                    if b:
                        far = jnp.exp(far - top)
                        total = total + jnp.sum(far, axis=-1, keepdims=True)
                    inv = 1.0 / total
                    res = dot((near * inv).astype(BF), qkv_ref[qrows, vc])
                    if b:
                        res = res + dot((far * inv).astype(BF), qkv_ref[0:upto, vc])
                    attn_ref[qrows, h * HEAD_DIM:(h + 1) * HEAD_DIM] = res.astype(BF)
                    lse_ref[qrows, h:h + 1] = top + jnp.log(total)

        send_ref[step] = dot(attn_ref[rows, :], wo_ref[...]).astype(BF)

        @pl.when(step > 0)
        def _():
            send(send_ref.at[step], recv_ref.at[step], asem, step, block).start()

    mixed = x_ref[...].astype(F32) + send_ref[0].astype(F32)
    for step in (1, 2, 3):
        send(send_ref.at[step], recv_ref.at[step], asem, step, partner(me, step)).wait_recv()
        mixed = mixed + recv_ref[step].astype(F32)
    if inside:
        gu_line.step(2)
    mixed_ref[...] = mixed
    n2 = (mixed * rms_factor(mixed) * gain_ref[1:2, :]).astype(BF)
    n2_ref[:, 0:d] = n2
    logits = dot(n2, ext_ref[...])
    named = named_ref[...] > 0.0
    top = jnp.max(jnp.where(named, logits, -1e30), axis=-1, keepdims=True)
    weight = jnp.where(named, jnp.exp(jnp.minimum(logits - top, 0.0)), 0.0)
    gates = weight / jnp.sum(weight, axis=-1, keepdims=True)
    gate_ref[...] = gates
    n2_ref[:, d:] = pack_two(gates, experts)
    gg.got_three()
    gg.finish()
    xg.finish()
    keep.wait()
    for step in (1, 2, 3):
        send(send_ref.at[step], recv_ref.at[step], asem, step, partner(me, step)).wait_send()
    if inside:
        wd_line.land()
        gu_line.land()
        for line in (qkv_line, wo_line, wd_line, gu_line):
            line.finish()
        qkv_spread.finish()
        gu_spread.finish()


def front(nq, nk, experts, x, g, named, weights, inside):
    toks, d = x.shape
    length = 4 * toks
    nqkv = nq + 2 * nk
    sds = jax.ShapeDtypeStruct
    out_shape = [
        sds((length, d), BF), sds((length, nqkv), BF), sds((length, nq), BF), sds((length, 128), F32),
        sds((toks, d), F32), sds((toks, d + 128), BF), sds((toks, 128), F32), sds((length, d), BF),
        sds((2, d), F32), sds((d, 128), BF),
    ]
    in_specs = [VM] * 5
    out_specs = [VM] * 10
    scratch = [
        pltpu.VMEM((length, d), BF), pltpu.VMEM((4, toks, d), BF), pltpu.VMEM((4, toks, d), BF),
        pltpu.SemaphoreType.DMA((2, 4)), pltpu.SemaphoreType.DMA((2, 4)), pltpu.SemaphoreType.DMA((2, 4)),
        pltpu.SemaphoreType.DMA((5,)),
    ]
    if inside:
        qkvo, guo, wdo, woo = weights
        in_specs = [VM] * 4 + [ANY] * 3
        out_shape += [
            sds((d, nqkv + 128), BF), sds((nq, d), BF), sds((4, 8) + guo.shape[1:], BF),
            sds((wdo.shape[0], 8) + wdo.shape[1:], BF),
        ]
        out_specs += [VM, VM, ANY, ANY]
        scratch += [
            pltpu.VMEM((4, 8) + qkvo.shape[1:], BF), pltpu.SemaphoreType.DMA((2, 2, 4)),
            pltpu.SemaphoreType.DMA((4, 2, 10)),
        ]
    return pl.pallas_call(
        functools.partial(front_kernel, nq, nk, experts, inside),
        name="front",
        out_shape=out_shape,
        in_specs=in_specs,
        out_specs=out_specs,
        scratch_shapes=scratch,
        compiler_params=pltpu.CompilerParams(collective_id=1, has_side_effects=True, vmem_limit_bytes=60 * MIB),
        cost_estimate=pl.CostEstimate(flops=20 * 10**9, bytes_accessed=60 * 10**6, transcendentals=4 * 10**6),
    )(x, g, named, *weights)


def moe_kernel(experts, shards, *refs):
    (n2o_ref, gs_ref, gu_hbm, wd_hbm) = refs[:4]
    if shards:
        grad_ref, refs = refs[4], refs[5:]
    else:
        ggu_ref, gwd_ref, refs = refs[4], refs[5], refs[6:]
    dn2_ref, hg_ref, n2_ref, gu_ref, wd_ref, dpre_ref, nsem, lsem = refs
    me = lax.axis_index("seq")
    toks, de = n2o_ref.shape
    d = de - 128
    ff = wd_ref.shape[0]
    fc = ff // experts
    load_gu = pltpu.make_async_copy(gu_hbm, gu_ref, lsem.at[0])
    load_wd = pltpu.make_async_copy(wd_hbm, wd_ref, lsem.at[1])
    load_gu.start()
    load_wd.start()
    greet(me, 0)
    ng = Gather(me, n2o_ref, n2_ref, nsem)
    ng.start()
    load_gu.wait()
    load_wd.wait()

    @pl.loop(0, 4)
    def _(step):
        block = partner(me, step)
        rows = pl.ds(pl.multiple_of(block * toks, toks), toks)

        @pl.when(step == 0)
        def _():
            n2_ref[rows, :] = n2o_ref[...]

        @pl.when(step == 1)
        def _():
            ng.got_one()

        @pl.when(step == 2)
        def _():
            ng.got_two()

        @pl.when(step == 3)
        def _():
            ng.got_three()

        def one_expert(e, dgate):
            cols = pl.ds(pl.multiple_of(e * 2 * fc, 2 * fc), 2 * fc)
            hcols = pl.ds(pl.multiple_of(e * fc, fc), fc)
            pre = dot(n2_ref[rows, 0:d], gu_ref[:, cols])
            dh0 = dot_t(gs_ref[rows, :], wd_ref[hcols, :])
            packed = n2_ref[rows, d:].astype(F32)
            lane = lanes(packed.shape)
            mine = (lane == e) | (lane == e + experts)
            gate = jnp.sum(jnp.where(mine, packed, 0.0), axis=-1, keepdims=True)
            gp, up = pre[:, 0:fc], pre[:, fc:]
            sig = 1.0 / (1.0 + jnp.exp(-gp))
            act = gp * sig
            hid = (act * up).astype(BF).astype(F32)
            hg_ref[rows, hcols] = (gate * hid).astype(BF)
            dh = gate * dh0
            dpre_ref[rows, pl.ds(pl.multiple_of(e * 2 * fc, fc), fc)] = (
                dh * up * sig * (1.0 + gp * (1.0 - sig))).astype(BF)
            dpre_ref[rows, pl.ds(pl.multiple_of(e * 2 * fc + fc, fc), fc)] = (dh * act).astype(BF)
            return dgate + jnp.where(lane == e, jnp.sum(hid * dh0, axis=-1, keepdims=True), 0.0)

        dgate = lax.fori_loop(0, experts, one_expert, jnp.zeros((toks, 128), F32))
        dn2_ref[step, :, d:] = pack_two(dgate, experts)
        tile = 512

        @pl.loop(0, d // tile)
        def _(t):
            cols = pl.ds(pl.multiple_of(t * tile, tile), tile)
            dn2_ref[step, :, cols] = dot_t(dpre_ref[rows, :], gu_ref[cols, :]).astype(BF)

    if shards:
        rows, wide = d // 4 // shards, 2 * fc

        @pl.loop(0, 4)
        def _(s):
            cols = pl.ds(pl.multiple_of(s * (d // 4), 128), d // 4)
            grad = t_dot(n2_ref[:, cols], dpre_ref[...]).astype(BF)
            for f in range(shards):
                for e in range(experts):
                    at = pl.ds(pl.multiple_of((s * experts + e) * rows, 16), rows)
                    grad_ref[f, at, :] = grad[f * rows:(f + 1) * rows, e * wide:(e + 1) * wide]

        lower = fc // shards
        parts = d // wide

        @pl.loop(0, experts)
        def _(e):
            cols = pl.ds(pl.multiple_of(e * fc, fc), fc)
            grad = t_dot(hg_ref[:, cols], gs_ref[...]).astype(BF)
            for f in range(shards):
                for c in range(parts):
                    at = pl.ds(pl.multiple_of(4 * experts * rows + (e * parts + c) * lower, 16), lower)
                    grad_ref[f, at, :] = grad[f * lower:(f + 1) * lower, c * wide:(c + 1) * wide]

    else:

        @pl.loop(0, d // 256)
        def _(t):
            cols = pl.ds(pl.multiple_of(t * 256, 256), 256)
            ggu_ref[cols, :] = t_dot(n2_ref[:, cols], dpre_ref[...]).astype(BF)

        @pl.loop(0, ff // 256)
        def _(t):
            cols = pl.ds(pl.multiple_of(t * 256, 256), 256)
            gwd_ref[cols, :] = t_dot(hg_ref[:, cols], gs_ref[...]).astype(BF)

    ng.finish()


def moe(experts, shards, n2o, gs, gu, wd):
    toks, de = n2o.shape
    d = de - 128
    length = 4 * toks
    ff = wd.shape[0]
    sds = jax.ShapeDtypeStruct
    wide = 2 * ff // experts
    if shards:
        grads = [sds((shards, 3 * ff * d // wide // shards, wide), BF)]
    else:
        grads = [sds((d, 2 * ff), BF), sds((ff, d), BF)]
    return pl.pallas_call(
        functools.partial(moe_kernel, experts, shards),
        name="moe",
        out_shape=grads + [sds((4, toks, de), BF), sds((length, ff), BF)],
        in_specs=[VM] * 2 + [ANY] * 2,
        out_specs=[VM] * (2 + len(grads)),
        scratch_shapes=[
            pltpu.VMEM((length, de), BF), pltpu.VMEM((d, 2 * ff), BF), pltpu.VMEM((ff, d), BF),
            pltpu.VMEM((length, 2 * ff), BF),
            pltpu.SemaphoreType.DMA((2, 4)), pltpu.SemaphoreType.DMA((2,)),
        ],
        compiler_params=pltpu.CompilerParams(collective_id=2, has_side_effects=True, vmem_limit_bytes=62 * MIB),
        cost_estimate=pl.CostEstimate(flops=40 * 10**9, bytes_accessed=80 * 10**6, transcendentals=4 * 10**6),
    )(n2o, gs, gu, wd)


def rest_kernel(nq, nk, experts, shards, *refs):
    (x_ref, g_ref, mixed_ref, gate_ref, n2o_ref, gain_ref, ext_ref, n1_ref, qkv_ref, attn_ref, lse_ref, wqkv_ref, wo_ref,
     dn2_ref, hg_ref, wd_ref) = refs[:16]
    out_ref, gin_ref = refs[16:18]
    if shards:
        grad_ref, refs = refs[18], refs[19:]
    else:
        gqkv_ref, gwo_ref, refs = refs[18], refs[19], refs[20:]
    (dmixed_ref, dproj_ref, dattn_ref, dqkv_ref, dk_ref, dv_ref, outp_ref, grouter_ref, send_ref, nrecv_ref, recv_ref,
     orecv_ref, nsem, psem, dsem, osem) = refs
    me = lax.axis_index("seq")
    toks, d = x_ref.shape
    group = nq // nk
    nqkv = nq + 2 * nk
    own = pl.ds(pl.multiple_of(me * toks, toks), toks)
    greet(me, 0)
    for step in (3, 2, 1):
        send(dn2_ref.at[step], nrecv_ref.at[step], nsem, step, partner(me, step)).start()

    @pl.loop(0, 4)
    def _(step):
        rows = pl.ds(pl.multiple_of(partner(me, step) * toks, toks), toks)
        outp_ref[step] = dot(hg_ref[rows, :], wd_ref[...]).astype(BF)

    total = dn2_ref[0].astype(F32)
    for step in (1, 2, 3):
        send(dn2_ref.at[step], nrecv_ref.at[step], nsem, step, partner(me, step)).wait_recv()
        total = total + nrecv_ref[step].astype(F32)
    both = total[:, d:]
    lane = lanes(both.shape)
    dgate = jnp.where(lane < experts, both + pltpu.roll(both, 128 - experts, 1), 0.0)
    gates = gate_ref[...]
    dlog = (gates * (dgate - jnp.sum(gates * dgate, axis=-1, keepdims=True))).astype(BF)
    dn = (total[:, 0:d] + dot_t(dlog, ext_ref[...])) * gain_ref[1:2, :]
    mixed = mixed_ref[...]
    r2 = rms_factor(mixed)
    dmixed = (
        g_ref[...].astype(F32) + r2 * dn - mixed * (r2 * r2 * r2) * jnp.mean(dn * mixed, axis=-1, keepdims=True))
    dmixed_ref[...] = dmixed
    dproj_ref[own, :] = dmixed.astype(BF)
    pg = Gather(me, dproj_ref.at[own], dproj_ref, psem)
    pg.start()
    grouter_ref[...] = pack_two(t_dot(n2o_ref[:, 0:d], dlog), experts)

    @pl.loop(0, 4)
    def _(step):
        rows = pl.ds(pl.multiple_of(partner(me, step) * toks, toks), toks)

        @pl.when(step == 1)
        def _():
            pg.got_one()

        @pl.when(step == 2)
        def _():
            pg.got_two()

        @pl.when(step == 3)
        def _():
            pg.got_three()

        dattn_ref[rows, :] = dot_t(dproj_ref[rows, :], wo_ref[...]).astype(BF)

    for step in (3, 2, 1):
        send(outp_ref.at[step], orecv_ref.at[step], osem, step, partner(me, step)).start()

    if shards:
        narrow = nqkv + 128
        part = nq // shards
        grad = t_dot(attn_ref[...], dproj_ref[...]).astype(BF)
        for f in range(shards):
            for c in range(d // narrow):
                at = 4 * (d // 4 // shards) + c * part
                grad_ref[f, at:at + part, :] = grad[f * part:(f + 1) * part, c * narrow:(c + 1) * narrow]
    else:

        @pl.loop(0, nq // 128)
        def _(t):
            cols = pl.ds(pl.multiple_of(t * 128, 128), 128)
            gwo_ref[cols, :] = t_dot(attn_ref[:, cols], dproj_ref[...]).astype(BF)

    dk_ref[...] = jnp.zeros_like(dk_ref)
    dv_ref[...] = jnp.zeros_like(dv_ref)
    for b in range(4):
        upto = b * toks
        qrows = slice(upto, upto + toks)
        inside = lanes((toks, toks)) <= lax.broadcasted_iota(jnp.int32, (toks, toks), 0)
        for h in range(nq // HEAD_DIM):
            g = h // group
            hc = slice(h * HEAD_DIM, (h + 1) * HEAD_DIM)
            gc = slice(g * HEAD_DIM, (g + 1) * HEAD_DIM)
            q = qkv_ref[qrows, hc] * SCALE
            da = dattn_ref[qrows, hc]
            lse = lse_ref[qrows, h:h + 1]
            parts = ([slice(0, upto)] if b else []) + [qrows]
            probs, dprobs = [], []
            delta = 0.0
            for krows in parts:
                k = qkv_ref[krows, nq + g * HEAD_DIM: nq + (g + 1) * HEAD_DIM]
                v = qkv_ref[krows, nq + nk + g * HEAD_DIM: nq + nk + (g + 1) * HEAD_DIM]
                p = jnp.exp(dot_t(q, k) - lse)
                if krows is qrows:
                    p = jnp.where(inside, p, 0.0)
                dp = dot_t(da, v)
                delta = delta + jnp.sum(p * dp, axis=-1, keepdims=True)
                probs.append(p)
                dprobs.append(dp)
            dq = 0.0
            for krows, p, dp in zip(parts, probs, dprobs):
                k = qkv_ref[krows, nq + g * HEAD_DIM: nq + (g + 1) * HEAD_DIM]
                ds = (p * (dp - delta)).astype(BF)
                dq = dq + dot(ds, k)
                dk_ref[krows, gc] += t_dot(ds, q)
                dv_ref[krows, gc] += t_dot(p.astype(BF), da)
            dqkv_ref[qrows, hc] = (dq * SCALE).astype(BF)
    dqkv_ref[:, nq:nq + nk] = dk_ref[...].astype(BF)
    dqkv_ref[:, nq + nk:] = dv_ref[...].astype(BF)

    @pl.loop(0, 4)
    def _(turn):
        step = 3 - turn
        block = partner(me, step)
        rows = pl.ds(pl.multiple_of(block * toks, toks), toks)
        send_ref[step] = dot_t(dqkv_ref[rows, :], wqkv_ref[:, 0:nqkv]).astype(BF)

        @pl.when(step > 0)
        def _():
            send(send_ref.at[step], recv_ref.at[step], dsem, step, block).start()

    if shards:
        part = d // 4 // shards

        @pl.loop(0, 4)
        def _(s):
            cols = pl.ds(pl.multiple_of(s * (d // 4), 128), d // 4)
            at = pl.ds(pl.multiple_of(s * part, 16), part)
            grad = t_dot(n1_ref[:, cols], dqkv_ref[...]).astype(BF)
            for f in range(shards):
                grad_ref[f, at, 0:nqkv] = grad[f * part:(f + 1) * part, :]
                of = pl.ds(pl.multiple_of(s * (d // 4) + f * part, 16), part)
                grad_ref[f, at, nqkv:] = grouter_ref[of, :]

    else:

        @pl.loop(0, d // 256)
        def _(t):
            cols = pl.ds(pl.multiple_of(t * 256, 256), 256)
            gqkv_ref[cols, 0:nqkv] = t_dot(n1_ref[:, cols], dqkv_ref[...]).astype(BF)

        gqkv_ref[:, nqkv:] = grouter_ref[...]

    out = mixed_ref[...] + outp_ref[0].astype(F32)
    for step in (1, 2, 3):
        send(outp_ref.at[step], orecv_ref.at[step], osem, step, partner(me, step)).wait_recv()
        out = out + orecv_ref[step].astype(F32)
    out_ref[...] = out.astype(BF)
    dn = send_ref[0].astype(F32)
    for step in (1, 2, 3):
        send(send_ref.at[step], recv_ref.at[step], dsem, step, partner(me, step)).wait_recv()
        dn = dn + recv_ref[step].astype(F32)
    dn = dn * gain_ref[0:1, :]
    xf = x_ref[...].astype(F32)
    r1 = rms_factor(xf)
    gin_ref[...] = (
        dmixed_ref[...] + r1 * dn - xf * (r1 * r1 * r1) * jnp.mean(dn * xf, axis=-1, keepdims=True)).astype(BF)
    pg.finish()
    for step in (1, 2, 3):
        send(dn2_ref.at[step], nrecv_ref.at[step], nsem, step, partner(me, step)).wait_send()
        send(send_ref.at[step], recv_ref.at[step], dsem, step, partner(me, step)).wait_send()
        send(outp_ref.at[step], orecv_ref.at[step], osem, step, partner(me, step)).wait_send()


def rest(nq, nk, experts, shards, *args):
    toks, d = args[0].shape
    length = 4 * toks
    nqkv = nq + 2 * nk
    sds = jax.ShapeDtypeStruct
    if shards:
        narrow = nqkv + 128
        grads = [sds((shards, d // shards + d // narrow * (nq // shards), narrow), BF)]
    else:
        grads = [sds((d, nqkv + 128), BF), sds((nq, d), BF)]
    sems = pltpu.SemaphoreType.DMA((2, 4))
    return pl.pallas_call(
        functools.partial(rest_kernel, nq, nk, experts, shards),
        name="rest",
        out_shape=[sds((toks, d), BF), sds((toks, d), BF)] + grads,
        in_specs=[VM] * 16,
        out_specs=[VM] * (2 + len(grads)),
        scratch_shapes=[
            pltpu.VMEM((toks, d), F32), pltpu.VMEM((length, d), BF), pltpu.VMEM((length, nq), BF),
            pltpu.VMEM((length, nqkv), BF), pltpu.VMEM((length, nk), F32), pltpu.VMEM((length, nk), F32),
            pltpu.VMEM((4, toks, d), BF), pltpu.VMEM((d, 128), BF), pltpu.VMEM((4, toks, d), BF),
            pltpu.VMEM((4, toks, d + 128), BF), pltpu.VMEM((4, toks, d), BF), pltpu.VMEM((4, toks, d), BF),
            sems, sems, sems, sems,
        ],
        compiler_params=pltpu.CompilerParams(collective_id=3, has_side_effects=True, vmem_limit_bytes=62 * MIB),
        cost_estimate=pl.CostEstimate(flops=60 * 10**9, bytes_accessed=80 * 10**6, transcendentals=4 * 10**6),
    )(*args)


def shards(x, cot, routes, gain_attn, w_query, w_key, w_value, w_out, gain_ffn, router, w_gate, w_up, w_down):
    n_seq = lax.axis_size("seq")
    n_fsdp = lax.axis_size("fsdp")
    rows, d = w_query.shape
    experts, ff_rows, _ = w_down.shape
    ff = w_gate.shape[2]
    fc = ff // n_seq

    nq, nk = w_query.shape[1] // n_seq, w_key.shape[1] // n_seq
    nqkv = nq + 2 * nk
    inside = n_seq == 4 and n_fsdp == 8 and rows % 16 == 0 and ff_rows % 16 == 0

    extra = jnp.concatenate(
        [router, gain_attn[:, None], gain_ffn[:, None], jnp.zeros((rows, 128 - 2 - experts), BF)], axis=1
    )
    qkv = jnp.concatenate(
        [w_query.reshape(rows, n_seq, -1), w_key.reshape(rows, n_seq, -1), w_value.reshape(rows, n_seq, -1),
         jnp.broadcast_to(extra[:, None], (rows, n_seq, 128))], axis=2,
    ).transpose(1, 0, 2)
    gu = jnp.stack([w_gate, w_up]).reshape(2, experts, rows, n_seq, fc).transpose(3, 2, 1, 0, 4)
    gu = gu.reshape(n_seq, rows, 2 * experts * fc)
    hot = routes[0][:, :, None] == jnp.arange(128)[None, None, :]
    named = jnp.any(hot, axis=1).astype(F32)
    if inside:
        (n1, proj, attn, lse, mixed, n2o, gates, gs, gains, ext, wqkv, wo, gu, wd) = front(
            nq, nk, experts, x[0], cot[0], named, (qkv, gu, w_down, w_out), True)
        gu = gu.reshape(d, -1)
        wd = wd.reshape(-1, d)
    else:
        qkv = lax.all_to_all(qkv, "seq", split_axis=0, concat_axis=0, tiled=True)
        gu = lax.all_to_all(gu, "seq", split_axis=0, concat_axis=0, tiled=True)
        do = jnp.concatenate([w_down.reshape(experts * ff_rows, d), w_out], axis=0)
        wqkv = lax.all_gather(qkv, "fsdp", axis=1).reshape(d, -1)
        do = lax.all_gather(do, "fsdp", axis=0)
        wo = do[:, experts * ff_rows:].reshape(-1, d)
        wd = do[:, : experts * ff_rows].reshape(n_fsdp, experts, ff_rows, d).transpose(1, 0, 2, 3).reshape(-1, d)
        gu = lax.all_gather(gu, "fsdp", axis=1).reshape(d, -1)
        (n1, proj, attn, lse, mixed, n2o, gates, gs, gains, ext) = front(
            nq, nk, experts, x[0], cot[0], named, (wqkv, wo), False)

    packed = n_fsdp if inside else 0
    *grads, dn2, hg = moe(experts, packed, n2o, gs, gu, wd)
    if inside:
        grad = lax.psum_scatter(grads[0], "fsdp", scatter_dimension=0, tiled=True)[0]
    else:
        ggu, gwd = grads
        gwd = gwd.reshape(experts, n_fsdp, ff_rows, d).transpose(1, 0, 2, 3).reshape(-1, d)
        gwd = lax.psum_scatter(gwd, "fsdp", scatter_dimension=0, tiled=True)
        ggu = ggu.reshape(n_seq, n_fsdp, rows, experts, 2 * fc).transpose(1, 0, 3, 2, 4)
        ggu = lax.psum_scatter(ggu, "fsdp", scatter_dimension=0, tiled=True).reshape(n_seq, experts * rows, 2 * fc)
    output, gin, *tail = rest(
        nq, nk, experts, packed, x[0], cot[0], mixed, gates, n2o, gains, ext, n1, proj, attn, lse, wqkv, wo, dn2, hg, wd)
    if inside:
        tail, grad = lax.optimization_barrier((tail[0], grad))
        tail = lax.psum_scatter(tail, "fsdp", scatter_dimension=0, tiled=True)[0]
        cut = n_seq * experts * rows
        ggu = grad[:cut].reshape(n_seq, experts * rows, 2 * fc)
        gwd = grad[cut:].reshape(experts, -1, ff_rows, 2 * fc).transpose(0, 2, 1, 3)
        gqkv = tail[: n_seq * rows].reshape(n_seq, rows, -1)
        gwo = tail[n_seq * rows:].reshape(-1, rows, nqkv + 128).transpose(1, 0, 2).reshape(rows, d)
    else:
        gqkv, gwo = tail
        gwo = lax.psum_scatter(gwo, "fsdp", scatter_dimension=0, tiled=True)
        gqkv = gqkv.reshape(n_seq, n_fsdp, rows, -1).transpose(1, 0, 2, 3).reshape(n_fsdp * n_seq * rows, -1)
        gqkv = lax.psum_scatter(gqkv, "fsdp", scatter_dimension=0, tiled=True).reshape(n_seq, rows, -1)
    ggu = lax.all_to_all(ggu, "seq", split_axis=0, concat_axis=0, tiled=True)
    gqkv = lax.all_to_all(gqkv, "seq", split_axis=0, concat_axis=0, tiled=True)

    gqkv = gqkv.astype(F32)
    g_query = gqkv[:, :, :nq].transpose(1, 0, 2).reshape(rows, -1)
    g_key = gqkv[:, :, nq: nq + nk].transpose(1, 0, 2).reshape(rows, -1)
    g_value = gqkv[:, :, nq + nk: nqkv].transpose(1, 0, 2).reshape(rows, -1)
    g_router = jnp.sum(gqkv[:, :, nqkv: nqkv + experts] + gqkv[:, :, nqkv + experts: nqkv + 2 * experts], axis=0)
    ggu = ggu.astype(F32).reshape(n_seq, experts, rows, 2, fc).transpose(3, 1, 2, 0, 4).reshape(2, experts, rows, ff)
    g_gate, g_up = ggu[0], ggu[1]
    g_gain_one = (
        jnp.sum(w_query.astype(F32) * g_query, axis=1) + jnp.sum(w_key.astype(F32) * g_key, axis=1)
        + jnp.sum(w_value.astype(F32) * g_value, axis=1)
    ) / gain_attn.astype(F32)
    g_gain_two = (
        jnp.sum(w_gate.astype(F32) * g_gate + w_up.astype(F32) * g_up, axis=(0, 2))
        + jnp.sum(router.astype(F32) * g_router, axis=1)
    ) / gain_ffn.astype(F32)
    return (
        output[None], gin[None], g_gain_one, g_query, g_key, g_value, gwo.astype(F32), g_gain_two, g_router,
        g_gate, g_up, gwd.astype(F32).reshape(experts, ff_rows, d),
    )


def solution(mesh):
    tok = P("fsdp", "seq", None)
    vec = P(("seq", "fsdp"))
    mat = P(("seq", "fsdp"), None)
    exp = P(None, ("seq", "fsdp"), None)
    return jax.shard_map(
        shards,
        mesh=mesh,
        in_specs=(tok, tok, tok, vec, mat, mat, mat, mat, vec, mat, exp, exp, exp),
        out_specs=(tok, tok, vec, mat, mat, mat, mat, vec, mat, exp, exp, exp),
        check_vma=False,
    )
```

time: 602 us -> 455 us (0.76)
  waiting for transfers between devices: 211 us -> 35.8 us
  Pallas kernels: 286 us -> 364 us
  blocking collectives: 24.9 us -> 0 us
  local copies, waits for them, and re-layouts: 40 us -> 19.9 us
    reduce_scatter x4 -> x2, waiting for transfers between devices: 156 us -> 22.7 us  [the longest x1 22.7 us: shards(): tail = lax.psum_scatter(tail, 'fsdp', scatter_dimension=0, tiled=True)[0]]
    pallas_call x3, Pallas kernels: 286 us -> 364 us  [the longest x1 152 us: front(): pl.pallas_call(functools.partial(front_kernel, nq, nk, experts, inside),...]
    all_gather x3 -> x0, waiting for transfers between devices: 55.3 us -> none  [the longest x1 42.8 us: shards(): do = lax.all_gather(do, 'fsdp', axis=0)]
    all_to_all x2 -> x0, blocking collectives: 24.9 us -> none  [the longest x1 13.5 us: shards(): gu = lax.all_to_all(gu, 'seq', split_axis=0, concat_axis=0, tiled=True)]
    reshape x4 -> x2, local copies, waits for them, and re-layouts: 13.7 us -> 1.8 us  [shards(): gwd.astype(F32).reshape(experts, ff_rows, d)]
    all_to_all x1, waiting for transfers between devices: 0.01 us -> 8.39 us  [shards(): ggu = lax.all_to_all(ggu, 'seq', split_axis=0, concat_axis=0, tiled=True)]
    slice x4 -> x5, local copies, waits for them, and re-layouts: 8.73 us -> 2.69 us  [the longest x1 1.73 us: shards(): gqkv = tail[:n_seq * rows].reshape(n_seq, rows, -1)]
  transfers between devices with their start and end apart: 9 -> 4, of which waited for: 6 -> 3; matrix products, arithmetic and copies ran while one was open for 6% -> 2% of each run, Pallas kernels for 17% -> 33%
where the time goes in v3:
time: 455 us; the launch traced here: 450 us
  Pallas kernels  364 us (80%)
  waiting for transfers between devices  35.8 us (8%)
  local copies, waits for them, and re-layouts  19.9 us (4%)
  between operations  14.5 us (3%)
  starting transfers between devices  7.75 us (2%)
  other arithmetic  7.25 us (2%)
    pallas_call x1, Pallas kernels, front(): pl.pallas_call(functools.partial(front_kernel, nq, nk, experts, inside),...  152 us
    pallas_call x1, Pallas kernels, rest(): pl.pallas_call(functools.partial(rest_kernel, nq, nk, experts, shards), n...  149 us
    pallas_call x1, Pallas kernels, moe(): pl.pallas_call(functools.partial(moe_kernel, experts, shards), name='moe'...  63.5 us
    reduce_scatter x1, waiting for transfers between devices, shards(): tail = lax.psum_scatter(tail, 'fsdp', scatter_dimension=0, tiled=True)[0]  22.7 us
  transfers between devices with their start and end apart: 4, of which 3 were waited for; matrix products, arithmetic and copies ran while one was open for 2% of the time, Pallas kernels for 33%

profile of v3, /device:TPU:0, one launch (start us, length us, event | category | flops | bytes accessed | tf_op | source)
XLA Modules:
  0.0 449.6 jit_solution(5351506059592902424)
XLA Ops:
  7.2 0.0 copy-start.3
  7.2 0.0 reduce-scatter.3.cloned.1.call-start
  7.2 0.9 fusion
  8.1 0.7 convert_element_type.50.refs_2_
  8.8 0.8 copy.71
  9.5 0.8 copy.70
  10.3 0.8 copy.69
  11.1 0.9 copy.103
  12.0 1.3 stack.10
  13.3 0.6 copy.76
  13.9 0.3 stack.9
  14.2 0.6 copy.75
  14.8 0.0 copy-start.9
  14.8 0.0 copy-start.10
  14.8 1.6 maximum_bitcast_fusion
  16.5 1.5 reshape.95.refs_4_
  18.0 0.1 pad.9.clone
  18.0 0.0 copy-done.10
  18.1 0.1 maximum_maximum_fusion
  18.2 0.7 maximum_bitcast_fusion.1.refs_3_
  18.9 151.6 %front.1 = (bf16[1024,1536]{1,0:T(8,128)(2,1)}, bf16[1024,640]{1,0:T(8,128)(2,1)}, bf16[1024,384]{1,0:T(8,128)(2,1)}, f32[1024,128]{1,0:T(8,128)}, f32[256,1536]...) custom-call(bf16[256,1536]{1,0:T(8,128)(2,1)} %bitcast.76, ...), custom_call_target="tpu_custom_call" | custom-call | flops 20000000000 | bytes 60000000 | tf_op jit(solution)/shard_map/front/pallas_call | solution.py:401
  170.5 63.5 %moe.1 = (bf16[8,1152,512]{2,1,0:T(8,128)(2,1)}, bf16[4,256,1664]{2,1,0:T(8,128)(2,1)}, bf16[1024,1024]{1,0:T(8,128)(2,1)}) custom-call(bf16[256,1664]{1,0:T(8,128)(2,1)} %get-tuple-element.36.refs_0_.refs_4_, bf16[1024,1536]{1,0:T(8,128)(2,1)} %get-tuple-element.45.refs_1_, bf16[1536,2048]{1,0:T(8,128)(2,1)} %bitcast.80, bf16[1024,1536]{1,0:T(8,128)(2,1)} %bitcast.81), custom_call_target="tpu_custom_call" | custom-call | flops 40000000000 | bytes 80000000 | tf_op jit(solution)/shard_map/moe/pallas_call | solution.py:535
  234.0 0.0 reduce-scatter.3.cloned.1.call-update
  234.0 0.0 reduce-scatter.5.cloned.1.call-start
  234.0 149.3 %rest.1 = (bf16[256,1536]{1,0:T(8,128)(2,1)}, bf16[256,1536]{1,0:T(8,128)(2,1)}, bf16[8,288,768]{2,1,0:T(8,128)(2,1)}) custom-call(bf16[256,1536]{1,0:T(8,128)(2,1)} %bitcast.77, bf16[256,1536]{1,0:T(8,128)(2,1)} %bitcast.79, f32[256,1536]{1,0:T(8,128)} %get-tuple-element.34.refs_2_, f32[256,128]{1,0:T(8,128)} %get-tuple-element.35.refs_3_, ...), custom_call_target="tpu_custom_call" | custom-call | flops 60000002048 | bytes 80000000 | tf_op jit(solution)/shard_map/rest/pallas_call | solution.py:733
  383.4 0.0 reduce-scatter.3.cloned.1.call-done
  383.4 0.0 reduce-scatter.5.cloned.1.call-update
  383.4 1.2 copy-done.4
  384.7 0.9 slice.42
  385.6 4.0 all-to-all-start.1
  389.7 0.1 copy.82
  389.8 0.3 copy.102
  390.1 1.5 reshape.108
  391.6 8.4 %all-to-all-done.1 = bf16[4,192,512]{2,1,0:T(8,128)(2,1)S(1)} async-done(((bf16[4,192,512]{2,1,0:T(8,128)(2,1)}), bf16[4,192,512]{2,1,0:T(8,128)(2,1)S(1)}, u32[]{:S(2)}, u32[]{:S(2)}) %all-to-all-start.1) | async-done | bytes 786464 | tf_op jit(solution)/shard_map/all_to_all | solution.py:816
  400.0 1.0 reshape.109
  401.0 1.0 copy.101
  402.0 0.3 fusion.2
  402.3 0.0 copy-start.2
  402.3 0.4 squeeze.22
  402.7 0.0 copy-start
  402.7 0.4 squeeze.21
  403.1 0.2 copy-done.2
  403.3 0.3 add_reduce_fusion
  403.6 22.7 %reduce-scatter.5.cloned.1.call-done = bf16[1,288,768]{2,1,0:T(8,128)(2,1)} async-done(((bf16[8,288,768]{2,1,0:T(8,128)(2,1)}), bf16[1,288,768]{2,1,0:T(8,128)(2,1)}) %reduce-scatter.5.cloned.1.call-update) | async-done | bytes 442384 | tf_op jit(solution)/shard_map/reduce_scatter | solution.py:805
  426.3 1.7 slice.48
  428.0 3.6 all-to-all-start
  431.7 0.7 copy.91
  432.4 4.7 %all-to-all-done = bf16[4,48,768]{2,1,0:T(8,128)(2,1)S(1)} async-done(((bf16[4,48,768]{2,1,0:T(8,128)(2,1)}), bf16[4,48,768]{2,1,0:T(8,128)(2,1)S(1)}, u32[]{:S(2)}, u32[]{:S(2)}) %all-to-all-start) | async-done | bytes 294944 | tf_op jit(solution)/shard_map/all_to_all | solution.py:817
  437.1 0.0 copy-start.13
  437.2 0.0 copy-start.12
  437.2 0.0 copy-start.7
  437.2 0.1 fusion.1
  437.3 0.0 copy-start.6
  437.3 0.8 multiply_reduce_fusion.1
  438.1 0.0 copy-start.5
  438.1 0.0 copy-done.8
  438.2 0.1 multiply_reduce_fusion
  438.3 0.8 multiply_reduce_fusion.2
  439.0 0.7 copy.84
  439.7 0.1 multiply_reduce_fusion.3
  439.8 0.5 convert_divide_fusion
  440.3 0.5 convert_divide_fusion.1
  440.9 0.9 copy.106
  441.8 0.9 copy.107
  (25 shorter events, 0.2 us)
Async XLA Ops:
  7.2 6.7 %copy-start.3 = (bf16[4,48,1024]{2,1,0:T(8,128)(2,1)S(1)}, bf16[4,48,1024]{2,1,0:T(8,128)(2,1)}, u32[]{:S(2)}) copy-start(bf16[4,48,1024]{2,1,0:T(8,128)(2,1)} %param.23) | copy-start | bytes 1179652
  7.2 376.2 %reduce-scatter.3.cloned.1.call-start = ((), (), s32[]{:S(2)}) async-start(), calls=%async_computation.4 | async-start | bytes 10616832 | tf_op jit(solution)/shard_map/reduce_scatter | solution.py:794
  14.8 3.2 copy-start.9
  14.8 3.2 copy-start.10
  234.0 192.3 %reduce-scatter.5.cloned.1.call-start = ((), (), s32[]{:S(2)}) async-start(), calls=%async_computation.5 | async-start | bytes 3981312 | tf_op jit(solution)/shard_map/reduce_scatter | solution.py:805
  383.4 1.3 copy-start.4
  384.7 5.0 %copy-start.11 = (bf16[48,4]{0,1:T(4,128)(2,1)S(1)}, bf16[48,4]{0,1:T(4,128)(2,1)}, u32[]{:S(2)}) copy-start(bf16[48,4]{0,1:T(4,128)(2,1)} %param.22) | copy-start | bytes 1156
  385.6 14.4 %all-to-all-start.1 = ((bf16[4,192,512]{2,1,0:T(8,128)(2,1)}), bf16[4,192,512]{2,1,0:T(8,128)(2,1)S(1)}, u32[]{:S(2)}, u32[]{:S(2)}) async-start(bf16[4,192,512]{2,1,0:T(8,128)(2,1)} %bitcast.18), calls=%async_computation.3 | async-start | bytes 1572864 | tf_op jit(solution)/shard_map/all_to_all | solution.py:816
  402.3 1.0 copy-start.2
  402.7 0.9 copy-start
  403.3 24.7 %copy-start.1 = (f32[4,48,1024]{2,1,0:T(8,128)}, f32[4,48,1024]{2,1,0:T(8,128)S(1)}, u32[]{:S(2)}) copy-start(f32[4,48,1024]{2,1,0:T(8,128)S(1)} %squeeze.21) | copy-start | bytes 2359300
  426.3 5.4 %slice-start = ((bf16[1,288,768]{2,1,0:T(8,128)(2,1)}), bf16[1,96,768]{2,1,0:T(8,128)(2,1)S(1)}, s32[]{:S(2)}) async-start(bf16[1,288,768]{2,1,0:T(8,128)(2,1)} %reduce-scatter.5.cloned.1.call-done), calls=%async_computation.6 | async-start | bytes 294912 | tf_op jit(solution)/shard_map/slice | solution.py:810
  428.0 9.1 %all-to-all-start = ((bf16[4,48,768]{2,1,0:T(8,128)(2,1)}), bf16[4,48,768]{2,1,0:T(8,128)(2,1)S(1)}, u32[]{:S(2)}, u32[]{:S(2)}) async-start(bf16[4,48,768]{2,1,0:T(8,128)(2,1)} %bitcast.12), calls=%async_computation.2 | async-start | bytes 589824 | tf_op jit(solution)/shard_map/all_to_all | solution.py:817
  432.4 5.7 %copy-start.8 = (bf16[48,1536]{1,0:T(8,128)(2,1)S(1)}, bf16[48,1536]{1,0:T(8,128)(2,1)}, u32[]{:S(2)}) copy-start(bf16[48,1536]{1,0:T(8,128)(2,1)} %param.17) | copy-start | bytes 442372
  437.1 2.7 copy-start.13
  437.2 3.2 copy-start.12
  437.2 3.7 copy-start.7
  437.3 4.4 copy-start.6
  438.1 4.5 %copy-start.5 = (f32[4,6,8,384]{3,2,0,1:T(8,128)}, f32[4,6,8,384]{3,2,0,1:T(8,128)S(1)}, u32[]{:S(2)}) copy-start(f32[4,6,8,384]{3,2,0,1:T(8,128)S(1)} %copy.88) | copy-start | bytes 884740
Sparse Core Ops, SparseCore 0:
  234.1 98.6 reduce-scatter.2
  383.6 42.6 reduce-scatter.4
